TPU v7x, 512 devices: a whole 4x8x8 slice. The times are simulated.
512 devices in a mesh: outer: 16 (over z, core), inner: 8 (over y), chan: 4 (over x).
Axes of the slice: x: 4, y: 8, z: 8, core: 2. Of those that a mesh axis runs over, the one named last changes fastest.
Arguments:
- q_stream: bfloat16 [16384, 4096], P(('outer', 'inner'), 'chan'), may hold values from -6 to 6
- k_stream: bfloat16 [16384, 4096], P(('outer', 'inner'), 'chan'), may hold values from -6 to 6
- v_stream: bfloat16 [16384, 4096], P(('outer', 'inner'), 'chan'), may hold values from -6 to 6
- filter_taps: bfloat16 [16384, 4096], P(('outer', 'inner'), 'chan'), may hold values from -0.046875 to 0.046875
- skip_gain: float32 [4096], P('chan'), may hold values from 0.3 to 1.5
- out_weight: bfloat16 [4096, 4096], P('chan', 'inner'), may hold values from -0.09375 to 0.09375
Outputs:
- layer_out: bfloat16 [16384, 4096], P(('outer', 'chan'), 'inner')
All inputs are finite; a program needn't handle non-finite values.
Results may differ from a plain program's by a relative error of at most 0.013.
Values may be sent and summed in bfloat16 or wider, within the bound.
A program may use at most 64 MiB of HBM per device.

v0:
```python
import jax
import jax.numpy as jnp
from jax import lax
from jax.sharding import PartitionSpec as P

two_pi = 6.283185307179586


def angle_table(left_ids, right_ids, modulus):
    index = left_ids[:, None] * right_ids[None, :] % modulus
    angles = index.astype(jnp.float32) * (two_pi / modulus)
    return (jnp.cos(angles), jnp.sin(angles))


def contract(form, table, values):
    return jnp.einsum(
        form, table, values, precision=lax.Precision.HIGHEST, preferred_element_type=jnp.float32
    )


def local(q_stream, k_stream, v_stream, filter_taps, skip_gain, out_weight):
    tok_rows, chan_cols = k_stream.shape
    outer_n = lax.axis_size("outer")
    inner_n = lax.axis_size("inner")
    slab_count = outer_n * inner_n
    per_slab = chan_cols // slab_count
    seq_len = slab_count * tok_rows
    total_len = 2 * seq_len
    fine_len = 128
    coarse_len = total_len // fine_len
    half_coarse = coarse_len // 2
    product = (k_stream.astype(jnp.float32) * v_stream.astype(jnp.float32)).astype(jnp.bfloat16)

    def to_blocks(values):
        return values.reshape(tok_rows, slab_count, per_slab).transpose(1, 2, 0)

    outgoing = jnp.stack([to_blocks(product), to_blocks(filter_taps)], axis=1)
    incoming = lax.all_to_all(outgoing, ("outer", "inner"), split_axis=0, concat_axis=0, tiled=True)
    signals = incoming.transpose(1, 2, 0, 3).astype(jnp.float32)
    coarse_ids = jnp.arange(coarse_len, dtype=jnp.int32)
    half_ids = jnp.arange(half_coarse, dtype=jnp.int32)
    fine_ids = jnp.arange(fine_len, dtype=jnp.int32)
    cos_coarse, sin_coarse = angle_table(coarse_ids, half_ids, coarse_len)
    cos_twist, sin_twist = angle_table(coarse_ids, fine_ids, total_len)
    cos_fine, sin_fine = angle_table(fine_ids, fine_ids, fine_len)
    section_real = contract("kn,scnm->sckm", cos_coarse, signals)
    section_imag = -contract("kn,scnm->sckm", sin_coarse, signals)
    twist_real = section_real * cos_twist + section_imag * sin_twist
    twist_imag = section_imag * cos_twist - section_real * sin_twist
    spec_real = contract("sckm,mj->sckj", twist_real, cos_fine) + contract(
        "sckm,mj->sckj", twist_imag, sin_fine
    )
    spec_imag = contract("sckm,mj->sckj", twist_imag, cos_fine) - contract(
        "sckm,mj->sckj", twist_real, sin_fine
    )
    prod_real = spec_real[0] * spec_real[1] - spec_imag[0] * spec_imag[1]
    prod_imag = spec_real[0] * spec_imag[1] + spec_imag[0] * spec_real[1]
    back_real = contract("ckj,jm->ckm", prod_real, cos_fine) - contract(
        "ckj,jm->ckm", prod_imag, sin_fine
    )
    back_imag = contract("ckj,jm->ckm", prod_imag, cos_fine) + contract(
        "ckj,jm->ckm", prod_real, sin_fine
    )
    turn_real = back_real * cos_twist - back_imag * sin_twist
    turn_imag = back_imag * cos_twist + back_real * sin_twist
    conv = contract("kn,ckm->cnm", cos_coarse, turn_real) - contract(
        "kn,ckm->cnm", sin_coarse, turn_imag
    )
    conv_out = (conv * (1.0 / total_len)).astype(jnp.bfloat16)
    conv_out = conv_out.transpose(1, 0, 2)
    conv_in = lax.all_to_all(conv_out, ("outer", "inner"), split_axis=0, concat_axis=0, tiled=True)
    conv_in = conv_in.reshape(chan_cols, tok_rows).T
    mixed = conv_in.astype(jnp.float32) + skip_gain[None, :] * product.astype(jnp.float32)
    gated = (q_stream.astype(jnp.float32) * mixed).astype(jnp.bfloat16)
    gathered = lax.all_gather(gated, "inner", axis=0, tiled=True)
    result = lax.psum_scatter(
        jnp.dot(gathered, out_weight, preferred_element_type=jnp.float32),
        "chan",
        scatter_dimension=0,
        tiled=True,
    )
    return result.astype(jnp.bfloat16)


def solution(mesh):
    return jax.shard_map(
        local,
        mesh=mesh,
        in_specs=(
            P(("outer", "inner"), "chan"),
            P(("outer", "inner"), "chan"),
            P(("outer", "inner"), "chan"),
            P(("outer", "inner"), "chan"),
            P("chan"),
            P("chan", "inner"),
        ),
        out_specs=P(("outer", "chan"), "inner"),
        check_vma=False,
    )
```

profile of v0, /device:TPU:1, one launch (start us, length us, event | category | flops | bytes accessed | tf_op | source)
XLA Modules:
  0.0 189.7 jit_solution(5418750411212124741)
XLA Ops:
  6.5 0.0 copy-start
  6.5 1.2 copy.31
  7.7 1.1 copy.32
  8.9 1.1 copy.33
  10.0 0.1 fusion.49
  10.1 0.1 pad_maximum_fusion
  10.1 0.9 copy.34
  11.0 18.6 %all-to-all-start = ((bf16[128,2,8,128]{3,2,1,0:T(8,128)(2,1)}), bf16[128,2,8,128]{3,2,1,0:T(8,128)(2,1)S(1)}, u32[]{:S(2)}, u32[]{:S(2)}) async-start(bf16[128,2,8,128]{3,2,1,0:T(8,128)(2,1)} %copy.34), calls=%async_computation | async-start | bytes 1048576 | tf_op jit(solution)/shard_map/all_to_all | solution.py:38
  29.7 0.5 fusion.63
  30.2 0.1 copy.42
  30.3 0.1 copy.43
  30.4 18.5 %all-to-all-done = bf16[128,2,8,128]{3,2,1,0:T(8,128)(2,1)S(1)} async-done(((bf16[128,2,8,128]{3,2,1,0:T(8,128)(2,1)}), bf16[128,2,8,128]{3,2,1,0:T(8,128)(2,1)S(1)}, u32[]{:S(2)}, u32[]{:S(2)}) %all-to-all-start) | async-done | bytes 524320 | tf_op jit(solution)/shard_map/all_to_all | solution.py:38
  48.9 0.5 copy.35
  49.3 1.5 fusion.20
  50.8 1.5 fusion.22
  52.3 3.9 %fusion.32 = f32[2,8,256,128]{3,2,1,0:T(8,128)S(1)} fusion(f32[2,8,128,256]{3,2,1,0:T(8,128)S(1)} %fusion.22, f32[2,8,128,256]{3,2,1,0:T(8,128)S(1)} %fusion.20, f32[256,128]{0,1:T(8,128)S(1)} %get-tuple-element.7, f32[256,128]{0,1:T(8,128)S(1)} %get-tuple-element.8), kind=kOutput, calls=%fused_computation.43 | convolution fusion | flops 807632896 | bytes 6553600 | tf_op jit(solution)/shard_map/sckm,mj->sckj/dot_general | solution.py:16
  56.2 3.9 %fusion.28 = f32[2,8,256,128]{3,2,1,0:T(8,128)S(1)} fusion(f32[2,8,128,256]{3,2,1,0:T(8,128)S(1)} %fusion.22, f32[2,8,128,256]{3,2,1,0:T(8,128)S(1)} %fusion.20, f32[256,128]{0,1:T(8,128)S(1)} %get-tuple-element.7, f32[256,128]{0,1:T(8,128)S(1)} %get-tuple-element.8), kind=kOutput, calls=%fused_computation.42 | convolution fusion | flops 807632896 | bytes 6553600 | tf_op jit(solution)/shard_map/sckm,mj->sckj/dot_general | solution.py:16
  60.1 4.1 %convolution_add_fusion = f32[2,8,256,128]{3,2,1,0:T(8,128)S(1)} fusion(f32[2,8,256,128]{3,2,1,0:T(8,128)S(1)} %fusion.32, f32[2,8,128,256]{3,2,1,0:T(8,128)S(1)} %fusion.22, f32[2,8,128,256]{3,2,1,0:T(8,128)S(1)} %fusion.20, f32[256,128]{0,1:T(8,128)S(1)} %get-tuple-element.7, f32[256,128]{0,1:T(8,128)S(1)} %get-tuple-element.8), kind=kOutput, calls=%fused_computation.7 | convolution fusion | flops 808157184 | bytes 8650752 | tf_op jit(solution)/shard_map/sckm,mj->sckj/dot_general | solution.py:16
  64.2 3.9 %convolution_subtract_fusion = f32[2,8,256,128]{3,2,1,0:T(8,128)S(1)} fusion(f32[2,8,256,128]{3,2,1,0:T(8,128)S(1)} %fusion.28, f32[2,8,128,256]{3,2,1,0:T(8,128)S(1)} %fusion.22, f32[2,8,128,256]{3,2,1,0:T(8,128)S(1)} %fusion.20, f32[256,128]{0,1:T(8,128)S(1)} %get-tuple-element.7, f32[256,128]{0,1:T(8,128)S(1)} %get-tuple-element.8), kind=kOutput, calls=%fused_computation.6 | convolution fusion | flops 808157184 | bytes 8650752 | tf_op jit(solution)/shard_map/sckm,mj->sckj/dot_general | solution.py:16
  68.1 0.2 multiply_subtract_fusion
  68.4 1.2 fusion.8
  69.6 1.2 fusion.4
  70.8 1.2 convolution_subtract_fusion.1
  72.1 1.5 convolution_add_fusion.1
  73.6 1.3 fusion.13
  74.9 0.0 copy-start.1
  74.9 0.0 copy-start.2
  74.9 1.3 fusion.3
  76.2 0.9 copy.44
  77.1 6.7 %all-to-all-start.1 = ((bf16[128,8,128]{2,1,0:T(8,128)(2,1)}), bf16[128,8,128]{2,1,0:T(8,128)(2,1)S(1)}, u32[]{:S(2)}, u32[]{:S(2)}) async-start(bf16[128,8,128]{2,1,0:T(8,128)(2,1)} %copy.44), calls=%async_computation.1 | async-start | bytes 524288 | tf_op jit(solution)/shard_map/all_to_all | solution.py:71
  83.8 0.0 all-gather.2.cloned.1.call-start
  83.9 0.0 copy-done.1
  83.9 0.2 copy.30
  84.0 14.5 %all-to-all-done.1 = bf16[128,8,128]{2,1,0:T(8,128)(2,1)S(1)} async-done(((bf16[128,8,128]{2,1,0:T(8,128)(2,1)}), bf16[128,8,128]{2,1,0:T(8,128)(2,1)S(1)}, u32[]{:S(2)}, u32[]{:S(2)}) %all-to-all-start.1) | async-done | bytes 262176 | tf_op jit(solution)/shard_map/all_to_all | solution.py:71
  98.5 0.0 copy-done.2
  98.5 0.9 fusion.19
  99.5 0.0 all-gather.2.cloned.1.call-update
  99.5 0.0 reduce-scatter.2.cloned.1.call-start
  99.5 38.9 %all-gather.2.cloned.1.call-done = bf16[1024,1024]{0,1:T(8,128)(2,1)} async-done(((bf16[128,1024]{0,1:T(8,128)(2,1)}), bf16[1024,1024]{0,1:T(8,128)(2,1)}) %all-gather.2.cloned.1.call-update) | async-done | bytes 2097168 | tf_op jit(solution)/shard_map/all_gather | solution.py:75
  138.4 0.0 copy-done
  138.4 4.2 %fusion.130 = f32[1024,512]{1,0:T(8,128)} fusion(bf16[1024,1024]{0,1:T(8,128)(2,1)} %all-gather.2.cloned.1.call-done, bf16[1024,512]{1,0:T(8,128)(2,1)S(1)} %copy-done), kind=kOutput, calls=%fused_computation.137 | convolution fusion | flops 1073741824 | bytes 5242880 | tf_op jit(solution)/shard_map/dot_general | solution.py:77
  142.7 0.0 reduce-scatter.2.cloned.1.call-update
  142.7 38.4 %reduce-scatter.2.cloned.1.call-done = f32[256,512]{1,0:T(8,128)} async-done(((f32[1024,512]{1,0:T(8,128)}), f32[256,512]{1,0:T(8,128)}) %reduce-scatter.2.cloned.1.call-update) | async-done | bytes 524304 | tf_op jit(solution)/shard_map/reduce_scatter | solution.py:76
  181.1 1.8 convert_element_type.105
Async XLA Ops:
  6.5 131.9 %copy-start = (bf16[1024,512]{1,0:T(8,128)(2,1)S(1)}, bf16[1024,512]{1,0:T(8,128)(2,1)}, u32[]{:S(2)}) copy-start(bf16[1024,512]{1,0:T(8,128)(2,1)} %param.11) | copy-start | bytes 3145732
  11.0 37.8 %all-to-all-start = ((bf16[128,2,8,128]{3,2,1,0:T(8,128)(2,1)}), bf16[128,2,8,128]{3,2,1,0:T(8,128)(2,1)S(1)}, u32[]{:S(2)}, u32[]{:S(2)}) async-start(bf16[128,2,8,128]{3,2,1,0:T(8,128)(2,1)} %copy.34), calls=%async_computation | async-start | bytes 1048576 | tf_op jit(solution)/shard_map/all_to_all | solution.py:38
  74.9 9.0 %copy-start.1 = (bf16[128,1024]{1,0:T(8,128)(2,1)S(1)}, bf16[128,1024]{1,0:T(8,128)(2,1)}, u32[]{:S(2)}) copy-start(bf16[128,1024]{1,0:T(8,128)(2,1)} %param.6) | copy-start | bytes 786436
  74.9 23.6 %copy-start.2 = (f32[1024]{0:T(1024)S(1)}, f32[1024]{0:T(1024)}, u32[]{:S(2)}) copy-start(f32[1024]{0:T(1024)} %param.10) | copy-start | bytes 12292
  77.1 21.4 %all-to-all-start.1 = ((bf16[128,8,128]{2,1,0:T(8,128)(2,1)}), bf16[128,8,128]{2,1,0:T(8,128)(2,1)S(1)}, u32[]{:S(2)}, u32[]{:S(2)}) async-start(bf16[128,8,128]{2,1,0:T(8,128)(2,1)} %copy.44), calls=%async_computation.1 | async-start | bytes 524288 | tf_op jit(solution)/shard_map/all_to_all | solution.py:71
  83.8 54.6 %all-gather.2.cloned.1.call-start = ((), (), s32[]{:S(2)}) async-start(), calls=%async_computation.3 | async-start | bytes 2359296 | tf_op jit(solution)/shard_map/all_gather | solution.py:75
  99.5 81.6 %reduce-scatter.2.cloned.1.call-start = ((), (), s32[]{:S(2)}) async-start(), calls=%async_computation.4 | async-start | bytes 2621440 | tf_op jit(solution)/shard_map/reduce_scatter | solution.py:76
Sparse Core Ops, SparseCore 0:
  99.6 38.7 all-gather.1
  142.8 38.2 reduce-scatter.1
where the time goes:
time: 190 us
  waiting for transfers between devices  110 us (58%)
  matrix products  30.7 us (16%)
  starting transfers between devices  25.4 us (13%)
  between operations  13.6 us (7%)
  local copies, waits for them, and re-layouts  6.06 us (3%)
  other arithmetic  3.6 us (2%)
    all_gather x1, waiting for transfers between devices, local(): gathered = lax.all_gather(gated, 'inner', axis=0, tiled=True)  38.9 us
    reduce_scatter x1, waiting for transfers between devices, local(): lax.psum_scatter(jnp.dot(gathered, out_weight, preferred_element_type=jnp...  38.4 us
    dot_general x12, matrix products, contract(): jnp.einsum(form, table, values, precision=lax.Precision.HIGHEST, preferre...  26.5 us
    all_to_all x1, starting transfers between devices, local(): lax.all_to_all(outgoing, ('outer', 'inner'), split_axis=0, concat_axis=0,...  18.6 us
    all_to_all x1, waiting for transfers between devices, local(): lax.all_to_all(outgoing, ('outer', 'inner'), split_axis=0, concat_axis=0,...  18.5 us
    all_to_all x1, waiting for transfers between devices, local(): lax.all_to_all(conv_out, ('outer', 'inner'), split_axis=0, concat_axis=0,...  14.5 us
    all_to_all x1, starting transfers between devices, local(): lax.all_to_all(conv_out, ('outer', 'inner'), split_axis=0, concat_axis=0,...  6.71 us
    dot_general x1, matrix products, local(): jnp.dot(gathered, out_weight, preferred_element_type=jnp.float32)  4.21 us
  transfers between devices with their start and end apart: 4, of which 4 were waited for; matrix products, arithmetic and copies ran while one was open for 0% of the time, Pallas kernels for 0%

commit v1 on v0

v1 whole, which is shorter than its diff:
```python
import functools

import jax
import jax.numpy as jnp
import numpy as np
from jax import lax
from jax.experimental import pallas as pl
from jax.experimental.pallas import tpu as pltpu
from jax.sharding import PartitionSpec as P

MESH = pl.DeviceIdType.MESH
F32 = jnp.float32
BF16 = jnp.bfloat16


def split_table(values):
    high = values.astype(np.float32).astype(jnp.bfloat16)
    low = (values - high.astype(np.float64)).astype(np.float32).astype(jnp.bfloat16)
    return high, low


@functools.lru_cache(maxsize=None)
def tables(slabs, tok):
    coarse = 2 * slabs
    total = coarse * tok
    rows = slabs + 1
    padded = -(-rows // 16) * 16
    k = np.arange(padded)
    live = (k < rows).astype(np.float64)
    angle = 2 * np.pi * ((k[:, None] * np.arange(slabs)[None, :]) % coarse) / coarse
    cos, sin = np.cos(angle) * live[:, None], np.sin(angle) * live[:, None]
    section = np.concatenate(split_table(np.concatenate([cos, -sin], axis=0)), axis=1)
    weight = np.where((k == 0) | (k == slabs), 1.0, 2.0) / total
    back = np.concatenate([(cos * weight[:, None]).T, (-sin * weight[:, None]).T], axis=1)
    back = np.stack(split_table(back))
    turn = 2 * np.pi * ((k[:, None] * np.arange(tok)[None, :]) % total) / total
    twist = np.stack([np.cos(turn), np.sin(turn)]).astype(np.float32)
    m = np.arange(tok)
    fine = 2 * np.pi * ((m[:, None] * m[None, :]) % tok) / tok
    c, s = np.cos(fine), np.sin(fine)
    forth = np.stack(split_table(np.block([[c, -s], [s, c]])))
    inverse = np.stack(split_table(np.block([[c, s], [-s, c]])))
    return section, twist, forth, inverse, back


def dot(a, b):
    return jnp.dot(a, b, preferred_element_type=F32)


def halves(x):
    high = x.astype(BF16)
    return high, (x - high.astype(F32)).astype(BF16)


def dot3(x, table):
    high, low = halves(x)
    return dot(high, table[0]) + (dot(high, table[1]) + dot(low, table[0]))


def near_first(n):
    order = [0]
    for d in range(1, n // 2):
        order += [d, n - d]
    return order + [n // 2]


def kernel(
    sizes,
    q_hbm, k_hbm, v_hbm, taps_hbm, skip_ref, w_hbm,
    section_ref, twist_ref, forth_ref, inverse_ref, back_ref,
    out_ref,
    k_buf, v_buf, taps_buf, w_buf,
    send1, recv1, recv2, signals, send2, recv3, conv_rows, skipped, q_recv, gated, send_part, recv_part,
    load_sem, y_send, y_recv, q_send, q_recv_sem, z_send, z_recv, b_send, b_recv, g_send, g_recv, p_send, p_recv,
):
    outer_n, inner_n, chan_n, tok, per = sizes
    block = outer_n * per
    o, i, c = lax.axis_index("outer"), lax.axis_index("inner"), lax.axis_index("chan")
    order = near_first(inner_n)
    waves = [(0, 1)]
    while waves[-1][1] < inner_n:
        low = waves[-1][1]
        waves.append((low, inner_n if low + 3 >= inner_n else low + 2))
    piece = inner_n * tok // chan_n
    hops = [2, 1, 3, 0] if chan_n == 4 else list(range(1, chan_n)) + [0]

    def at_inner(d):
        return lax.rem(i + d, inner_n)

    def at_outer(r):
        return lax.rem(o + r, outer_n)

    def at_chan(d):
        return lax.rem(c + d, chan_n)

    def cols(index):
        return pl.ds(pl.multiple_of(index * block, block), block)

    barrier = pltpu.get_barrier_semaphore()
    for d in range(1, inner_n):
        pl.semaphore_signal(barrier, inc=1, device_id={"inner": at_inner(d)}, device_id_type=MESH)
    for r in range(1, outer_n):
        pl.semaphore_signal(barrier, inc=1, device_id={"outer": at_outer(r)}, device_id_type=MESH)
    for d in range(1, chan_n):
        pl.semaphore_signal(barrier, inc=1, device_id={"chan": at_chan(d)}, device_id_type=MESH)

    loads = [
        pltpu.make_async_copy(k_hbm, k_buf, load_sem.at[0]),
        pltpu.make_async_copy(v_hbm, v_buf, load_sem.at[1]),
        pltpu.make_async_copy(taps_hbm, taps_buf, load_sem.at[2]),
        pltpu.make_async_copy(w_hbm, w_buf, load_sem.at[3]),
        pltpu.make_async_copy(q_hbm.at[:, cols(i)], q_recv.at[i], load_sem.at[4]),
    ]
    for load in loads:
        load.start()
    for load in loads[:3]:
        load.wait()

    def pack(index):
        span = cols(index)
        product = (k_buf[:, span].astype(F32) * v_buf[:, span].astype(F32)).astype(BF16).astype(F32)
        product = product.T.reshape(outer_n, per, tok)
        taps = taps_buf[:, span].astype(F32).T.reshape(outer_n, per, tok)
        return jnp.concatenate([product, taps], axis=1).astype(BF16)

    def y_copy(slot, d):
        return pltpu.make_async_remote_copy(
            src_ref=send1.at[slot], dst_ref=recv1.at[order.index((inner_n - d) % inner_n)],
            send_sem=y_send.at[slot], recv_sem=y_recv.at[order.index((inner_n - d) % inner_n)],
            device_id={"inner": at_inner(d)}, device_id_type=MESH,
        )

    recv1[0] = pack(i)
    for slot in range(1, inner_n):
        send1[slot] = pack(at_inner(order[slot]))
        if slot == 1:
            pl.semaphore_wait(barrier, inner_n + outer_n + chan_n - 3)
        y_copy(slot, order[slot]).start()

    def z_copy(wave, r):
        low, high = waves[wave]
        return pltpu.make_async_remote_copy(
            src_ref=recv1.at[pl.ds(low, high - low), at_outer(r)],
            dst_ref=recv2.at[o, pl.ds(low, high - low)],
            send_sem=z_send.at[wave, r], recv_sem=z_recv.at[wave, outer_n - r],
            device_id={"outer": at_outer(r)}, device_id_type=MESH,
        )

    def z_arrival(wave, r):
        low, high = waves[wave]
        here = recv2.at[at_outer(r), pl.ds(low, high - low)]
        return pltpu.make_async_remote_copy(
            src_ref=here, dst_ref=here,
            send_sem=z_send.at[wave, r], recv_sem=z_recv.at[wave, r],
            device_id={"outer": at_outer(r)}, device_id_type=MESH,
        )

    def q_copy(d):
        return pltpu.make_async_remote_copy(
            src_ref=q_hbm.at[:, cols(at_inner(d))], dst_ref=q_recv.at[i],
            send_sem=q_send.at[d], recv_sem=q_recv_sem.at[inner_n - d],
            device_id={"inner": at_inner(d)}, device_id_type=MESH,
        )

    for wave, (low, high) in enumerate(waves):
        for slot in range(low, high):
            if slot > 0:
                y_copy(slot, (inner_n - order[slot]) % inner_n).wait_recv()

        def z_start(r, carry, wave=wave):
            z_copy(wave, r).start()
            return carry

        lax.fori_loop(1, outer_n, z_start, 0)
    for d in order[1:]:
        q_copy(d).start()

    gain = skip_ref[:, cols(i)]
    for slot in range(inner_n):
        both = recv1[slot].astype(F32)
        product = both[:, :per].reshape(block, tok).T
        at = pl.multiple_of(at_inner(order[slot]) * tok, tok)
        skipped[pl.ds(at, tok), :] = product * gain

    for wave, (low, high) in enumerate(waves):

        def z_wait(r, carry, wave=wave):
            z_arrival(wave, r).wait_recv()
            return carry

        lax.fori_loop(1, outer_n, z_wait, 0)
        for slot in range(low, high):
            recv2[o, slot] = recv1[slot, o]
        for slot in range(low, high):
            place = at_inner(order[slot])
            for source in range(outer_n):
                row = pl.multiple_of((source * inner_n + place) * (2 * per), 2 * per)
                signals[pl.ds(row, 2 * per), :] = recv2[source, slot].astype(F32)

    slabs = outer_n * inner_n
    padded = twist_ref.shape[1]
    cos_twist, sin_twist = twist_ref[0], twist_ref[1]

    def wide(table, times):
        return jnp.concatenate([table] * times, axis=1)

    def convolve(first):
        both = []
        for channel in (first, first + 1):
            for kind in range(2):
                both.append(signals[pl.ds(channel + kind * per, slabs, stride=2 * per), :].astype(BF16))
        x = jnp.concatenate(both, axis=1)
        y = dot(section_ref[...], jnp.concatenate([x, x], axis=0))
        real, imag = y[:padded], y[padded:]
        cos4, sin4 = wide(cos_twist, 4), wide(sin_twist, 4)
        turned_real = real * cos4 + imag * sin4
        turned_imag = imag * cos4 - real * sin4
        stacked = jnp.concatenate(
            [
                jnp.concatenate([t[:, n * tok : (n + 1) * tok] for t in (turned_real, turned_imag)], axis=1)
                for n in range(4)
            ],
            axis=0,
        )
        spec = dot3(stacked, forth_ref)
        prods = []
        for n in range(2):
            a = spec[2 * n * padded : (2 * n + 1) * padded]
            b = spec[(2 * n + 1) * padded : (2 * n + 2) * padded]
            ar, ai, br, bi = a[:, :tok], a[:, tok:], b[:, :tok], b[:, tok:]
            prods.append(jnp.concatenate([ar * br - ai * bi, ar * bi + ai * br], axis=1))
        ret = dot3(jnp.concatenate(prods, axis=0), inverse_ref)
        ups = []
        for n in range(2):
            r = ret[n * padded : (n + 1) * padded]
            rr, ri = r[:, :tok], r[:, tok:]
            ups.append(
                jnp.concatenate([rr * cos_twist - ri * sin_twist, ri * cos_twist + rr * sin_twist], axis=0)
            )
        high, low = halves(jnp.concatenate(ups, axis=1))
        conv = dot(back_ref[0], high) + (dot(back_ref[1], high) + dot(back_ref[0], low))
        conv = [conv[:, n * tok : (n + 1) * tok].reshape(outer_n, inner_n, tok) for n in range(2)]
        return jnp.concatenate(conv, axis=1).astype(BF16)

    for pair in range(per // 2):
        send2[:, pl.ds(pair * 2 * inner_n, 2 * inner_n), :] = convolve(2 * pair)

    def b_copy(r):
        return pltpu.make_async_remote_copy(
            src_ref=send2.at[at_outer(r)], dst_ref=recv3.at[o],
            send_sem=b_send.at[r], recv_sem=b_recv.at[outer_n - r],
            device_id={"outer": at_outer(r)}, device_id_type=MESH,
        )

    def b_arrival(r):
        here = recv3.at[at_outer(r)]
        return pltpu.make_async_remote_copy(
            src_ref=here, dst_ref=here, send_sem=b_send.at[r], recv_sem=b_recv.at[r],
            device_id={"outer": at_outer(r)}, device_id_type=MESH,
        )

    def b_start(r, carry):
        b_copy(r).start()
        return carry

    def b_wait(r, carry):
        b_arrival(r).wait_recv()
        return carry

    lax.fori_loop(1, outer_n, b_start, 0)
    recv3[o] = send2[o]
    loads[3].wait()
    loads[4].wait()
    for d in range(1, inner_n):
        q_copy(inner_n - d).wait_recv()
    lax.fori_loop(1, outer_n, b_wait, 0)

    for source in range(outer_n):
        conv_rows[pl.ds(source * per * inner_n, per * inner_n), :] = recv3[source].astype(F32)
    for slab in range(inner_n):
        conv = conv_rows[pl.ds(slab, block, stride=inner_n), :].T
        span = pl.ds(slab * tok, tok)
        gated[i, span, :] = (q_recv[slab].astype(F32) * (conv + skipped[span, :])).astype(BF16)

    def reach(way, u):
        longer = inner_n // 2
        return longer if (u + way) % 2 == 0 else inner_n - 1 - longer

    def tokens_of(u):
        return pl.ds(pl.multiple_of(at_chan(hops[u]) * piece, piece), piece)

    def g_copy(way, u, r):
        step = 1 if way == 0 else inner_n - 1
        source = at_inner((inner_n - step) * (r - 1) % inner_n)
        part = gated.at[source, tokens_of(u)]
        return pltpu.make_async_remote_copy(
            src_ref=part, dst_ref=part,
            send_sem=g_send.at[way, u, r - 1], recv_sem=g_recv.at[way, u, r - 1],
            device_id={"inner": at_inner(step)}, device_id_type=MESH,
        )

    def g_arrival(way, u, r):
        step = 1 if way == 0 else inner_n - 1
        source = at_inner((inner_n - step) * r % inner_n)
        part = gated.at[source, tokens_of(u)]
        return pltpu.make_async_remote_copy(
            src_ref=part, dst_ref=part,
            send_sem=g_send.at[way, u, r - 1], recv_sem=g_recv.at[way, u, r - 1],
            device_id={"inner": at_inner(step)}, device_id_type=MESH,
        )

    def p_copy(u):
        return pltpu.make_async_remote_copy(
            src_ref=send_part.at[u], dst_ref=recv_part.at[u],
            send_sem=p_send.at[u], recv_sem=p_recv.at[u],
            device_id={"chan": at_chan(hops[u])}, device_id_type=MESH,
        )

    longest = inner_n // 2
    events = {}
    for u in range(chan_n):
        for r in range(1, longest + 2):
            events.setdefault(2 * u + r, []).append((u, r))
    for key in sorted(events):
        for u, r in events[key]:
            for way in range(2):
                if 1 < r <= reach(way, u) + 1:
                    g_arrival(way, u, r - 1).wait_recv()
                if r <= reach(way, u):
                    g_copy(way, u, r).start()
            if r == longest + 1:
                left = jnp.concatenate([gated[n, tokens_of(u), :] for n in range(inner_n)], axis=1)
                part = dot(left, w_buf[...])
                if u < chan_n - 1:
                    send_part[u] = part.astype(BF16)
                    p_copy(u).start()
                else:
                    total = part
                    for n in range(chan_n - 1):
                        p_copy(n).wait_recv()
                        total = total + recv_part[n].astype(F32)
                    out_ref[...] = total.astype(BF16)

    for slot in range(1, inner_n):
        y_copy(slot, order[slot]).wait_send()
    for d in range(1, inner_n):
        q_copy(d).wait_send()

    def sent(r, carry):
        for wave in range(len(waves)):
            z_copy(wave, r).wait_send()
        b_copy(r).wait_send()
        return carry

    lax.fori_loop(1, outer_n, sent, 0)
    for u in range(chan_n):
        for way in range(2):
            for r in range(1, reach(way, u) + 1):
                g_copy(way, u, r).wait_send()
        if u < chan_n - 1:
            p_copy(u).wait_send()


def local(q_stream, k_stream, v_stream, filter_taps, skip_gain, out_weight):
    tok, chans = k_stream.shape
    outer_n, inner_n, chan_n = (lax.axis_size(a) for a in ("outer", "inner", "chan"))
    slabs = outer_n * inner_n
    per = chans // slabs
    block = outer_n * per
    width = out_weight.shape[1]
    coarse = inner_n * tok
    piece = coarse // chan_n
    held = tables(slabs, tok)
    sizes = (outer_n, inner_n, chan_n, tok, per)
    waves = max(2, inner_n // 2)
    dma = pltpu.SemaphoreType.DMA
    any_spec, vmem = pl.BlockSpec(memory_space=pl.ANY), pl.BlockSpec(memory_space=pltpu.VMEM)
    return pl.pallas_call(
        functools.partial(kernel, sizes),
        out_shape=jax.ShapeDtypeStruct((piece, width), BF16),
        in_specs=[any_spec] * 4 + [vmem, any_spec] + [vmem] * 5,
        out_specs=vmem,
        scratch_shapes=[
            pltpu.VMEM((tok, chans), BF16),
            pltpu.VMEM((tok, chans), BF16),
            pltpu.VMEM((tok, chans), BF16),
            pltpu.VMEM((chans, width), BF16),
            pltpu.VMEM((inner_n, outer_n, 2 * per, tok), BF16),
            pltpu.VMEM((inner_n, outer_n, 2 * per, tok), BF16),
            pltpu.VMEM((outer_n, inner_n, 2 * per, tok), BF16),
            pltpu.VMEM((slabs * 2 * per, tok), F32),
            pltpu.VMEM((outer_n, per * inner_n, tok), BF16),
            pltpu.VMEM((outer_n, per * inner_n, tok), BF16),
            pltpu.VMEM((outer_n * per * inner_n, tok), F32),
            pltpu.VMEM((coarse, block), F32),
            pltpu.VMEM((inner_n, tok, block), BF16),
            pltpu.VMEM((inner_n, coarse, block), BF16),
            pltpu.VMEM((chan_n - 1, piece, width), BF16),
            pltpu.VMEM((chan_n - 1, piece, width), BF16),
            dma((5,)),
            dma((inner_n,)),
            dma((inner_n,)),
            dma((inner_n,)),
            dma((inner_n,)),
            dma((waves, outer_n)),
            dma((waves, outer_n)),
            dma((outer_n,)),
            dma((outer_n,)),
            dma((2, chan_n, inner_n // 2)),
            dma((2, chan_n, inner_n // 2)),
            dma((chan_n - 1,)),
            dma((chan_n - 1,)),
        ],
        compiler_params=pltpu.CompilerParams(
            collective_id=0, has_side_effects=True, vmem_limit_bytes=40 * 1024 * 1024
        ),
    )(q_stream, k_stream, v_stream, filter_taps, skip_gain[None, :], out_weight, *(jnp.asarray(t) for t in held))


def solution(mesh):
    return jax.shard_map(
        local,
        mesh=mesh,
        in_specs=(
            P(("outer", "inner"), "chan"),
            P(("outer", "inner"), "chan"),
            P(("outer", "inner"), "chan"),
            P(("outer", "inner"), "chan"),
            P("chan"),
            P("chan", "inner"),
        ),
        out_specs=P(("outer", "chan"), "inner"),
        check_vma=False,
    )
```

time: 190 us -> 104 us (0.55)
  the two profiles are of different devices: /device:TPU:1 before, /device:TPU:14 now
where the time goes in v1:
time: 104 us
  Pallas kernels  92.7 us (89%)
  local copies, waits for them, and re-layouts  11.1 us (11%)
    pallas_call x1, Pallas kernels, local(): pl.pallas_call(functools.partial(kernel, sizes), out_shape=jax.ShapeDtype...  92.7 us
    unnamed x23, local copies, waits for them, and re-layouts  11.1 us

profile of v1, /device:TPU:14, one launch (start us, length us, event | category | flops | bytes accessed | tf_op | source)
XLA Modules:
  0.0 103.8 jit_solution(11426060705716453074)
XLA Ops:
  0.0 0.0 copy-start
  0.0 1.2 %copy-done = bf16[1024,512]{1,0:T(8,128)(2,1)S(1)} copy-done((bf16[1024,512]{1,0:T(8,128)(2,1)S(1)}, bf16[1024,512]{1,0:T(8,128)(2,1)}, u32[]{:S(2)}) %copy-start) | copy-done | bytes 1048600
  1.2 0.0 copy-start.1
  1.2 0.9 copy-done.1
  2.2 0.0 copy-start.2
  2.2 0.9 copy-done.2
  3.1 0.0 copy-start.3
  3.1 0.9 copy-done.3
  4.1 0.0 copy-start.4
  4.1 0.9 copy-done.4
  5.0 0.0 copy-start.5
  5.0 0.9 copy-done.5
  6.0 0.0 copy-start.6
  6.0 0.9 copy-done.6
  6.9 0.0 copy-start.7
  6.9 0.9 copy-done.7
  7.9 0.0 copy-start.8
  7.9 0.9 copy-done.8
  8.8 0.0 copy-start.9
  8.8 0.9 copy-done.9
  9.7 0.0 copy-start.10
  9.7 0.7 copy-done.10
  10.4 92.7 %shard_map.109 = bf16[256,512]{1,0:T(8,128)(2,1)S(1)} custom-call(bf16[128,1024]{1,0:T(8,128)(2,1)S(1)} %copy-done.1, bf16[128,1024]{1,0:T(8,128)(2,1)S(1)} %copy-done.2, bf16[128,1024]{1,0:T(8,128)(2,1)S(1)} %copy-done.3, bf16[128,1024]{1,0:T(8,128)(2,1)S(1)} %copy-done.4, f32[1,1024]{1,0:T(1,128)S(1)} %bitcast.1, bf16[1024,512]{1,0:T(8,128)(2,1)S(1)} %copy-done, ...), custom_call_target="tpu_custom_call" | custom-call | tf_op jit(solution)/shard_map/pallas_call | solution.py:378
  103.1 0.7 copy.13
Async XLA Ops:
  0.0 1.2 %copy-start = (bf16[1024,512]{1,0:T(8,128)(2,1)S(1)}, bf16[1024,512]{1,0:T(8,128)(2,1)}, u32[]{:S(2)}) copy-start(bf16[1024,512]{1,0:T(8,128)(2,1)} %w_hbm.1) | copy-start | bytes 3145732
  1.2 0.9 copy-start.1
  2.2 0.9 copy-start.2
  3.1 0.9 copy-start.3
  4.1 0.9 copy-start.4
  5.0 0.9 copy-start.5
  6.0 0.9 copy-start.6
  6.9 0.9 copy-start.7
  7.9 0.9 copy-start.8
  8.8 0.9 copy-start.9
  9.7 0.7 copy-start.10

commit v2 on v1

--- a/solution.py
+++ b/solution.py
@@ -11,6 +11,8 @@
 MESH = pl.DeviceIdType.MESH
 F32 = jnp.float32
 BF16 = jnp.bfloat16
+PARTS = 4
+RING_LAG = 0.6
 
 
 def split_table(values):
@@ -66,15 +68,19 @@
 
 def kernel(
     sizes,
-    q_hbm, k_hbm, v_hbm, taps_hbm, skip_ref, w_hbm,
-    section_ref, twist_ref, forth_ref, inverse_ref, back_ref,
+    q_hbm, k_hbm, v_hbm, taps_hbm, skip_hbm, w_hbm,
+    section_hbm, twist_hbm, forth_hbm, inverse_hbm, back_hbm,
     out_ref,
-    k_buf, v_buf, taps_buf, w_buf,
-    send1, recv1, recv2, signals, send2, recv3, conv_rows, skipped, q_recv, gated, send_part, recv_part,
-    load_sem, y_send, y_recv, q_send, q_recv_sem, z_send, z_recv, b_send, b_recv, g_send, g_recv, p_send, p_recv,
+    k_buf, v_buf, taps_buf, skip_ref, w_buf, section_ref, twist_ref, forth_ref, inverse_ref, back_ref,
+    send1, recv1, recv2, signals, send2, recv3, conv_rows, q_recv, folded_p, folded_q, gate_p, gate_q,
+    gx, gated, w_rows, weights, total,
+    load_sem, y_send, y_recv, q_send, q_recv_sem, z_send, z_recv, b_send, b_recv, x_send, x_recv,
+    g_send, g_recv, w_send, w_recv, f_send, f_recv,
 ):
-    outer_n, inner_n, chan_n, tok, per = sizes
+    outer_n, inner_n, chan_n, tok, per, parts = sizes
+    slabs = outer_n * inner_n
     block = outer_n * per
+    each = per // parts
     o, i, c = lax.axis_index("outer"), lax.axis_index("inner"), lax.axis_index("chan")
     order = near_first(inner_n)
     waves = [(0, 1)]
@@ -82,7 +88,9 @@
         low = waves[-1][1]
         waves.append((low, inner_n if low + 3 >= inner_n else low + 2))
     piece = inner_n * tok // chan_n
-    hops = [2, 1, 3, 0] if chan_n == 4 else list(range(1, chan_n)) + [0]
+    near = inner_n // chan_n
+    core = lax.rem(o, 2)
+    sibling = o + 1 - 2 * core
 
     def at_inner(d):
         return lax.rem(i + d, inner_n)
@@ -108,8 +116,14 @@
         pltpu.make_async_copy(k_hbm, k_buf, load_sem.at[0]),
         pltpu.make_async_copy(v_hbm, v_buf, load_sem.at[1]),
         pltpu.make_async_copy(taps_hbm, taps_buf, load_sem.at[2]),
-        pltpu.make_async_copy(w_hbm, w_buf, load_sem.at[3]),
-        pltpu.make_async_copy(q_hbm.at[:, cols(i)], q_recv.at[i], load_sem.at[4]),
+        pltpu.make_async_copy(q_hbm.at[:, cols(i)], q_recv.at[i], load_sem.at[3]),
+        pltpu.make_async_copy(skip_hbm, skip_ref, load_sem.at[4]),
+        pltpu.make_async_copy(section_hbm, section_ref, load_sem.at[5]),
+        pltpu.make_async_copy(twist_hbm, twist_ref, load_sem.at[6]),
+        pltpu.make_async_copy(forth_hbm, forth_ref, load_sem.at[7]),
+        pltpu.make_async_copy(inverse_hbm, inverse_ref, load_sem.at[8]),
+        pltpu.make_async_copy(back_hbm, back_ref, load_sem.at[9]),
+        pltpu.make_async_copy(w_hbm, w_buf, load_sem.at[10]),
     ]
     for load in loads:
         load.start()
@@ -162,25 +176,61 @@
             device_id={"inner": at_inner(d)}, device_id_type=MESH,
         )
 
-    for wave, (low, high) in enumerate(waves):
-        for slot in range(low, high):
-            if slot > 0:
-                y_copy(slot, (inner_n - order[slot]) % inner_n).wait_recv()
-
-        def z_start(r, carry, wave=wave):
+    def z_start(wave):
+        def start(r, carry):
             z_copy(wave, r).start()
             return carry
 
-        lax.fori_loop(1, outer_n, z_start, 0)
+        lax.fori_loop(1, outer_n, start, 0)
+
+    z_start(0)
+
+    for load in loads[3:]:
+        load.wait()
+    for n in range(w_rows.shape[0]):
+        span = pl.ds(n * w_rows.shape[2], w_rows.shape[2])
+        w_rows[n] = w_buf[:, span].astype(F32)
+        for cc in range(per):
+            rows = w_rows[n, pl.ds(cc, slabs, stride=per), :]
+            weights[c, cc // each, span, pl.ds(cc % each * slabs, slabs)] = rows.T.astype(BF16)
+    mine = pl.ds(core * (parts // 2), parts // 2)
+
+    def w_copy(d):
+        held = weights.at[c, mine]
+        return pltpu.make_async_remote_copy(
+            src_ref=held, dst_ref=held, send_sem=w_send.at[d], recv_sem=w_recv.at[chan_n - d],
+            device_id={"chan": at_chan(d)}, device_id_type=MESH,
+        )
+
+    def f_copy(d, half):
+        held = weights.at[at_chan(d), pl.ds(half * (parts // 2), parts // 2)]
+        return pltpu.make_async_remote_copy(
+            src_ref=held, dst_ref=held, send_sem=f_send.at[d], recv_sem=f_recv.at[d],
+            device_id={"outer": sibling}, device_id_type=MESH,
+        )
+
+    for d in range(1, chan_n):
+        w_copy(d).start()
+
+    gain = jnp.broadcast_to(skip_ref[:, cols(i)], (tok, block)).T
+
+    def keep_product(slot):
+        both = recv1[slot].astype(F32)
+        rows = pl.ds(slot * block, block)
+        folded_p[rows, :] = both[:, :per].reshape(block, tok) * gain
+        place = at_inner(order[slot])
+        for cc in range(per):
+            gate_p[cc, place] = folded_p[pl.ds(slot * block + cc, outer_n, stride=per), :]
+
+    for wave, (low, high) in enumerate(waves):
+        if wave > 0:
+            for slot in range(low, high):
+                y_copy(slot, (inner_n - order[slot]) % inner_n).wait_recv()
+            z_start(wave)
+        for slot in range(low, high):
+            keep_product(slot)
     for d in order[1:]:
         q_copy(d).start()
-
-    gain = skip_ref[:, cols(i)]
-    for slot in range(inner_n):
-        both = recv1[slot].astype(F32)
-        product = both[:, :per].reshape(block, tok).T
-        at = pl.multiple_of(at_inner(order[slot]) * tok, tok)
-        skipped[pl.ds(at, tok), :] = product * gain
 
     for wave, (low, high) in enumerate(waves):
 
@@ -197,7 +247,6 @@
                 row = pl.multiple_of((source * inner_n + place) * (2 * per), 2 * per)
                 signals[pl.ds(row, 2 * per), :] = recv2[source, slot].astype(F32)
 
-    slabs = outer_n * inner_n
     padded = twist_ref.shape[1]
     cos_twist, sin_twist = twist_ref[0], twist_ref[1]
 
@@ -242,104 +291,114 @@
         conv = [conv[:, n * tok : (n + 1) * tok].reshape(outer_n, inner_n, tok) for n in range(2)]
         return jnp.concatenate(conv, axis=1).astype(BF16)
 
-    for pair in range(per // 2):
-        send2[:, pl.ds(pair * 2 * inner_n, 2 * inner_n), :] = convolve(2 * pair)
-
-    def b_copy(r):
-        return pltpu.make_async_remote_copy(
-            src_ref=send2.at[at_outer(r)], dst_ref=recv3.at[o],
-            send_sem=b_send.at[r], recv_sem=b_recv.at[outer_n - r],
+    def part_rows(h):
+        return pl.ds(h * each * inner_n, each * inner_n)
+
+    def b_copy(h, r):
+        return pltpu.make_async_remote_copy(
+            src_ref=send2.at[at_outer(r), part_rows(h)], dst_ref=recv3.at[o, part_rows(h)],
+            send_sem=b_send.at[h, r], recv_sem=b_recv.at[h, outer_n - r],
             device_id={"outer": at_outer(r)}, device_id_type=MESH,
         )
 
-    def b_arrival(r):
-        here = recv3.at[at_outer(r)]
-        return pltpu.make_async_remote_copy(
-            src_ref=here, dst_ref=here, send_sem=b_send.at[r], recv_sem=b_recv.at[r],
+    def b_arrival(h, r):
+        here = recv3.at[at_outer(r), part_rows(h)]
+        return pltpu.make_async_remote_copy(
+            src_ref=here, dst_ref=here, send_sem=b_send.at[h, r], recv_sem=b_recv.at[h, r],
             device_id={"outer": at_outer(r)}, device_id_type=MESH,
         )
 
-    def b_start(r, carry):
-        b_copy(r).start()
-        return carry
-
-    def b_wait(r, carry):
-        b_arrival(r).wait_recv()
-        return carry
-
-    lax.fori_loop(1, outer_n, b_start, 0)
+    for h in range(parts):
+        for pair in range(h * each // 2, (h + 1) * each // 2):
+            send2[:, pl.ds(pair * 2 * inner_n, 2 * inner_n), :] = convolve(2 * pair)
+
+        def b_start(r, carry, h=h):
+            b_copy(h, r).start()
+            return carry
+
+        lax.fori_loop(1, outer_n, b_start, 0)
     recv3[o] = send2[o]
-    loads[3].wait()
-    loads[4].wait()
+
     for d in range(1, inner_n):
         q_copy(inner_n - d).wait_recv()
-    lax.fori_loop(1, outer_n, b_wait, 0)
-
-    for source in range(outer_n):
-        conv_rows[pl.ds(source * per * inner_n, per * inner_n), :] = recv3[source].astype(F32)
     for slab in range(inner_n):
-        conv = conv_rows[pl.ds(slab, block, stride=inner_n), :].T
-        span = pl.ds(slab * tok, tok)
-        gated[i, span, :] = (q_recv[slab].astype(F32) * (conv + skipped[span, :])).astype(BF16)
-
-    def reach(way, u):
-        longer = inner_n // 2
-        return longer if (u + way) % 2 == 0 else inner_n - 1 - longer
-
-    def tokens_of(u):
-        return pl.ds(pl.multiple_of(at_chan(hops[u]) * piece, piece), piece)
-
-    def g_copy(way, u, r):
+        folded_q[pl.ds(slab * block, block), :] = q_recv[slab].astype(F32).T
+        for cc in range(per):
+            gate_q[cc, slab] = folded_q[pl.ds(slab * block + cc, outer_n, stride=per), :]
+
+    def x_copy(h, d):
+        return pltpu.make_async_remote_copy(
+            src_ref=gx.at[h, at_chan(d)], dst_ref=gated.at[h, c, :, i],
+            send_sem=x_send.at[h, d], recv_sem=x_recv.at[h, chan_n - d],
+            device_id={"chan": at_chan(d)}, device_id_type=MESH,
+        )
+
+    for h in range(parts):
+
+        def b_wait(r, carry, h=h):
+            b_arrival(h, r).wait_recv()
+            return carry
+
+        lax.fori_loop(1, outer_n, b_wait, 0)
+        count = each * inner_n
+        first = h * outer_n * count
+        for source in range(outer_n):
+            conv_rows[pl.ds(first + source * count, count), :] = recv3[source, part_rows(h), :].astype(F32)
+        for e in range(each):
+            cc = h * each + e
+            for slab in range(inner_n):
+                conv = conv_rows[pl.ds(first + e * inner_n + slab, outer_n, stride=count), :]
+                value = (gate_q[cc, slab] * (conv + gate_p[cc, slab])).astype(BF16)
+                gx[h, slab // near, e, :, pl.ds(slab % near * tok, tok)] = value
+        for d in range(1, chan_n):
+            x_copy(h, d).start()
+        gated[h, c, :, i] = gx[h, c]
+
+    for d in range(1, chan_n):
+        w_copy(chan_n - d).wait_recv()
+        f_copy(d, core).start()
+
+    longest = inner_n // 2
+
+    def reach(way, h):
+        return longest if (h + way) % 2 == 0 else inner_n - 1 - longest
+
+    def g_copy(way, h, r, arrival=False):
         step = 1 if way == 0 else inner_n - 1
-        source = at_inner((inner_n - step) * (r - 1) % inner_n)
-        part = gated.at[source, tokens_of(u)]
-        return pltpu.make_async_remote_copy(
-            src_ref=part, dst_ref=part,
-            send_sem=g_send.at[way, u, r - 1], recv_sem=g_recv.at[way, u, r - 1],
+        source = at_inner((inner_n - step) * (r if arrival else r - 1) % inner_n)
+        held = gated.at[h, :, :, source]
+        return pltpu.make_async_remote_copy(
+            src_ref=held, dst_ref=held,
+            send_sem=g_send.at[way, h, r - 1], recv_sem=g_recv.at[way, h, r - 1],
             device_id={"inner": at_inner(step)}, device_id_type=MESH,
         )
 
-    def g_arrival(way, u, r):
-        step = 1 if way == 0 else inner_n - 1
-        source = at_inner((inner_n - step) * r % inner_n)
-        part = gated.at[source, tokens_of(u)]
-        return pltpu.make_async_remote_copy(
-            src_ref=part, dst_ref=part,
-            send_sem=g_send.at[way, u, r - 1], recv_sem=g_recv.at[way, u, r - 1],
-            device_id={"inner": at_inner(step)}, device_id_type=MESH,
-        )
-
-    def p_copy(u):
-        return pltpu.make_async_remote_copy(
-            src_ref=send_part.at[u], dst_ref=recv_part.at[u],
-            send_sem=p_send.at[u], recv_sem=p_recv.at[u],
-            device_id={"chan": at_chan(hops[u])}, device_id_type=MESH,
-        )
-
-    longest = inner_n // 2
-    events = {}
-    for u in range(chan_n):
+    events = []
+    for h in range(parts):
         for r in range(1, longest + 2):
-            events.setdefault(2 * u + r, []).append((u, r))
-    for key in sorted(events):
-        for u, r in events[key]:
-            for way in range(2):
-                if 1 < r <= reach(way, u) + 1:
-                    g_arrival(way, u, r - 1).wait_recv()
-                if r <= reach(way, u):
-                    g_copy(way, u, r).start()
-            if r == longest + 1:
-                left = jnp.concatenate([gated[n, tokens_of(u), :] for n in range(inner_n)], axis=1)
-                part = dot(left, w_buf[...])
-                if u < chan_n - 1:
-                    send_part[u] = part.astype(BF16)
-                    p_copy(u).start()
-                else:
-                    total = part
-                    for n in range(chan_n - 1):
-                        p_copy(n).wait_recv()
-                        total = total + recv_part[n].astype(F32)
-                    out_ref[...] = total.astype(BF16)
+            events.append((RING_LAG * h + r, h, r))
+    for _, h, r in sorted(events):
+        if r == 1:
+            for d in range(1, chan_n):
+                x_copy(h, chan_n - d).wait_recv()
+        for way in range(2):
+            if 1 < r <= reach(way, h) + 1:
+                g_copy(way, h, r - 1, arrival=True).wait_recv()
+            if r <= reach(way, h):
+                g_copy(way, h, r).start()
+        if r == longest + 1:
+            if h == 0:
+                for d in range(1, chan_n):
+                    f_copy(d, 1 - core).wait_recv()
+            part = None
+            for group in range(chan_n):
+                left, right = weights[group, h], gated[h, group].reshape(each * slabs, near * tok)
+                term = dot(left, right)
+                part = term if part is None else part + term
+            if h < parts - 1:
+                total[...] = part if h == 0 else total[...] + part
+            else:
+                out_ref[...] = (total[...] + part).T.astype(BF16)
 
     for slot in range(1, inner_n):
         y_copy(slot, order[slot]).wait_send()
@@ -349,16 +408,20 @@
     def sent(r, carry):
         for wave in range(len(waves)):
             z_copy(wave, r).wait_send()
-        b_copy(r).wait_send()
+        for h in range(parts):
+            b_copy(h, r).wait_send()
         return carry
 
     lax.fori_loop(1, outer_n, sent, 0)
-    for u in range(chan_n):
+    for d in range(1, chan_n):
+        w_copy(d).wait_send()
+        f_copy(d, core).wait_send()
+        for h in range(parts):
+            x_copy(h, d).wait_send()
+    for h in range(parts):
         for way in range(2):
-            for r in range(1, reach(way, u) + 1):
-                g_copy(way, u, r).wait_send()
-        if u < chan_n - 1:
-            p_copy(u).wait_send()
+            for r in range(1, reach(way, h) + 1):
+                g_copy(way, h, r).wait_send()
 
 
 def local(q_stream, k_stream, v_stream, filter_taps, skip_gain, out_weight):
@@ -371,20 +434,25 @@
     coarse = inner_n * tok
     piece = coarse // chan_n
     held = tables(slabs, tok)
-    sizes = (outer_n, inner_n, chan_n, tok, per)
+    parts = PARTS
+    each = per // parts
+    lanes = min(width, 128)
+    sizes = (outer_n, inner_n, chan_n, tok, per, parts)
     waves = max(2, inner_n // 2)
     dma = pltpu.SemaphoreType.DMA
-    any_spec, vmem = pl.BlockSpec(memory_space=pl.ANY), pl.BlockSpec(memory_space=pltpu.VMEM)
+    hbm = pl.BlockSpec(memory_space=pltpu.HBM)
     return pl.pallas_call(
         functools.partial(kernel, sizes),
         out_shape=jax.ShapeDtypeStruct((piece, width), BF16),
-        in_specs=[any_spec] * 4 + [vmem, any_spec] + [vmem] * 5,
-        out_specs=vmem,
+        in_specs=[hbm] * 11,
+        out_specs=pl.BlockSpec(memory_space=pltpu.VMEM),
         scratch_shapes=[
             pltpu.VMEM((tok, chans), BF16),
             pltpu.VMEM((tok, chans), BF16),
             pltpu.VMEM((tok, chans), BF16),
+            pltpu.VMEM((1, chans), F32),
             pltpu.VMEM((chans, width), BF16),
+            *(pltpu.VMEM(t.shape, t.dtype) for t in held),
             pltpu.VMEM((inner_n, outer_n, 2 * per, tok), BF16),
             pltpu.VMEM((inner_n, outer_n, 2 * per, tok), BF16),
             pltpu.VMEM((outer_n, inner_n, 2 * per, tok), BF16),
@@ -392,27 +460,36 @@
             pltpu.VMEM((outer_n, per * inner_n, tok), BF16),
             pltpu.VMEM((outer_n, per * inner_n, tok), BF16),
             pltpu.VMEM((outer_n * per * inner_n, tok), F32),
-            pltpu.VMEM((coarse, block), F32),
             pltpu.VMEM((inner_n, tok, block), BF16),
-            pltpu.VMEM((inner_n, coarse, block), BF16),
-            pltpu.VMEM((chan_n - 1, piece, width), BF16),
-            pltpu.VMEM((chan_n - 1, piece, width), BF16),
-            dma((5,)),
+            pltpu.VMEM((inner_n * block, tok), F32),
+            pltpu.VMEM((inner_n * block, tok), F32),
+            pltpu.VMEM((per, inner_n, outer_n, tok), F32),
+            pltpu.VMEM((per, inner_n, outer_n, tok), F32),
+            pltpu.VMEM((parts, chan_n, each, outer_n, piece), BF16),
+            pltpu.VMEM((parts, chan_n, each, inner_n, outer_n, piece), BF16),
+            pltpu.VMEM((width // lanes, chans, lanes), F32),
+            pltpu.VMEM((chan_n, parts, width, each * slabs), BF16),
+            pltpu.VMEM((width, piece), F32),
+            dma((11,)),
             dma((inner_n,)),
             dma((inner_n,)),
             dma((inner_n,)),
             dma((inner_n,)),
             dma((waves, outer_n)),
             dma((waves, outer_n)),
-            dma((outer_n,)),
-            dma((outer_n,)),
-            dma((2, chan_n, inner_n // 2)),
-            dma((2, chan_n, inner_n // 2)),
-            dma((chan_n - 1,)),
-            dma((chan_n - 1,)),
+            dma((parts, outer_n)),
+            dma((parts, outer_n)),
+            dma((parts, chan_n)),
+            dma((parts, chan_n)),
+            dma((2, parts, inner_n // 2)),
+            dma((2, parts, inner_n // 2)),
+            dma((chan_n,)),
+            dma((chan_n,)),
+            dma((chan_n,)),
+            dma((chan_n,)),
         ],
         compiler_params=pltpu.CompilerParams(
-            collective_id=0, has_side_effects=True, vmem_limit_bytes=40 * 1024 * 1024
+            collective_id=0, has_side_effects=True, vmem_limit_bytes=60 * 1024 * 1024
         ),
     )(q_stream, k_stream, v_stream, filter_taps, skip_gain[None, :], out_weight, *(jnp.asarray(t) for t in held))
 

time: 104 us -> 78.2 us (0.75)
  the two profiles are of different devices: /device:TPU:14 before, /device:TPU:20 now
where the time goes in v2:
time: 78.2 us; the launch traced here: 78.1 us
  Pallas kernels  76.4 us (98%)
  local copies, waits for them, and re-layouts  1.67 us (2%)
    pallas_call x1, Pallas kernels, local(): pl.pallas_call(functools.partial(kernel, sizes), out_shape=jax.ShapeDtype...  76.4 us
    unnamed x1, local copies, waits for them, and re-layouts  1.67 us

profile of v2, /device:TPU:20, one launch (start us, length us, event | category | flops | bytes accessed | tf_op | source)
XLA Modules:
  0.0 78.1 jit_solution(15500265570639087111)
XLA Ops:
  0.0 76.4 %shard_map.109 = bf16[256,512]{1,0:T(8,128)(2,1)} custom-call(bf16[128,1024]{1,0:T(8,128)(2,1)} %q_hbm.1, bf16[128,1024]{1,0:T(8,128)(2,1)} %k_hbm.1, bf16[128,1024]{1,0:T(8,128)(2,1)} %v_hbm.1, bf16[128,1024]{1,0:T(8,128)(2,1)} %taps_hbm.1, f32[1,1024]{1,0:T(1,128)} %bitcast.1, bf16[1024,512]{1,0:T(8,128)(2,1)} %w_hbm.1, ...), custom_call_target="tpu_custom_call" | custom-call | tf_op jit(solution)/shard_map/pallas_call | solution.py:444
  76.4 1.7 %copy.13 = bf16[256,512]{1,0:T(8,128)(2,1)} copy(bf16[256,512]{1,0:T(8,128)(2,1)} %shard_map.109) | data formatting | bytes 524288

commit v3 on v2

--- a/solution.py
+++ b/solution.py
@@ -12,7 +12,9 @@
 F32 = jnp.float32
 BF16 = jnp.bfloat16
 PARTS = 4
-RING_LAG = 0.6
+RING_LAG = 0.3
+Q_AT = 4
+PASS_AT = 3
 
 
 def split_table(values):
@@ -45,6 +47,13 @@
     return section, twist, forth, inverse, back
 
 
+def pick_table(outer_n, per):
+    block = outer_n * per
+    device, signal, channel = np.meshgrid(np.arange(outer_n), np.arange(2), np.arange(per), indexing="ij")
+    column = (signal * block + device * per + channel).reshape(-1)
+    return (column[:, None] == np.arange(2 * block)[None, :]).astype(np.float32).astype(jnp.bfloat16)
+
+
 def dot(a, b):
     return jnp.dot(a, b, preferred_element_type=F32)
 
@@ -69,12 +78,12 @@
 def kernel(
     sizes,
     q_hbm, k_hbm, v_hbm, taps_hbm, skip_hbm, w_hbm,
-    section_hbm, twist_hbm, forth_hbm, inverse_hbm, back_hbm,
+    section_hbm, twist_hbm, forth_hbm, inverse_hbm, back_hbm, pick_hbm,
     out_ref,
-    k_buf, v_buf, taps_buf, skip_ref, w_buf, section_ref, twist_ref, forth_ref, inverse_ref, back_ref,
-    send1, recv1, recv2, signals, send2, recv3, conv_rows, q_recv, folded_p, folded_q, gate_p, gate_q,
+    k_buf, v_buf, taps_buf, skip_ref, w_buf, section_ref, twist_ref, forth_ref, inverse_ref, back_ref, pick_ref,
+    send1, recv2, signals, send2, recv3, conv_rows, q_recv, gains, folded, gate_q,
     gx, gated, w_rows, weights, total,
-    load_sem, y_send, y_recv, q_send, q_recv_sem, z_send, z_recv, b_send, b_recv, x_send, x_recv,
+    load_sem, ready, d_send, d_recv, q_send, q_recv_sem, b_send, b_recv, x_send, x_recv,
     g_send, g_recv, w_send, w_recv, f_send, f_recv,
 ):
     outer_n, inner_n, chan_n, tok, per, parts = sizes
@@ -83,11 +92,6 @@
     each = per // parts
     o, i, c = lax.axis_index("outer"), lax.axis_index("inner"), lax.axis_index("chan")
     order = near_first(inner_n)
-    waves = [(0, 1)]
-    while waves[-1][1] < inner_n:
-        low = waves[-1][1]
-        waves.append((low, inner_n if low + 3 >= inner_n else low + 2))
-    piece = inner_n * tok // chan_n
     near = inner_n // chan_n
     core = lax.rem(o, 2)
     sibling = o + 1 - 2 * core
@@ -116,6 +120,7 @@
         pltpu.make_async_copy(k_hbm, k_buf, load_sem.at[0]),
         pltpu.make_async_copy(v_hbm, v_buf, load_sem.at[1]),
         pltpu.make_async_copy(taps_hbm, taps_buf, load_sem.at[2]),
+        pltpu.make_async_copy(pick_hbm, pick_ref, load_sem.at[11]),
         pltpu.make_async_copy(q_hbm.at[:, cols(i)], q_recv.at[i], load_sem.at[3]),
         pltpu.make_async_copy(skip_hbm, skip_ref, load_sem.at[4]),
         pltpu.make_async_copy(section_hbm, section_ref, load_sem.at[5]),
@@ -127,47 +132,51 @@
     ]
     for load in loads:
         load.start()
-    for load in loads[:3]:
+    pl.semaphore_wait(barrier, inner_n + outer_n + chan_n - 3)
+    for r in range(1, outer_n):
+        pl.semaphore_signal(ready, inc=1, device_id={"outer": at_outer(r)}, device_id_type=MESH)
+    for load in loads[:4]:
         load.wait()
 
     def pack(index):
         span = cols(index)
-        product = (k_buf[:, span].astype(F32) * v_buf[:, span].astype(F32)).astype(BF16).astype(F32)
-        product = product.T.reshape(outer_n, per, tok)
-        taps = taps_buf[:, span].astype(F32).T.reshape(outer_n, per, tok)
-        return jnp.concatenate([product, taps], axis=1).astype(BF16)
-
-    def y_copy(slot, d):
-        return pltpu.make_async_remote_copy(
-            src_ref=send1.at[slot], dst_ref=recv1.at[order.index((inner_n - d) % inner_n)],
-            send_sem=y_send.at[slot], recv_sem=y_recv.at[order.index((inner_n - d) % inner_n)],
-            device_id={"inner": at_inner(d)}, device_id_type=MESH,
-        )
-
-    recv1[0] = pack(i)
+        product = (k_buf[:, span].astype(F32) * v_buf[:, span].astype(F32)).astype(BF16)
+        both = jnp.concatenate([product, taps_buf[:, span]], axis=1)
+        rows = lax.dot_general(pick_ref[...], both, (((1,), (1,)), ((), ())), preferred_element_type=F32)
+        return rows.reshape(outer_n, 2 * per, tok).astype(BF16)
+
+    def d_copy(slot, r):
+        there = order.index((inner_n - order[slot]) % inner_n)
+        return pltpu.make_async_remote_copy(
+            src_ref=send1.at[slot, at_outer(r)], dst_ref=recv2.at[o, there],
+            send_sem=d_send.at[slot], recv_sem=d_recv.at[there],
+            device_id={"outer": at_outer(r), "inner": at_inner(order[slot])}, device_id_type=MESH,
+        )
+
+    def d_all(slot):
+        held = recv2.at[pl.ds(0, outer_n - 1 if slot == 0 else outer_n), slot]
+        return pltpu.make_async_remote_copy(
+            src_ref=held, dst_ref=held, send_sem=d_send.at[slot], recv_sem=d_recv.at[slot],
+            device_id={"outer": sibling}, device_id_type=MESH,
+        )
+
+    def d_start(slot, first):
+        def start(r, carry):
+            d_copy(slot, r).start()
+            return carry
+
+        lax.fori_loop(first, outer_n, start, 0)
+
+    for slot in range(inner_n):
+        send1[slot] = pack(at_inner(order[slot]))
+        if slot == 0:
+            d_start(0, 1)
+        else:
+            d_copy(slot, 0).start()
+    pl.semaphore_wait(ready, outer_n - 1)
     for slot in range(1, inner_n):
-        send1[slot] = pack(at_inner(order[slot]))
-        if slot == 1:
-            pl.semaphore_wait(barrier, inner_n + outer_n + chan_n - 3)
-        y_copy(slot, order[slot]).start()
-
-    def z_copy(wave, r):
-        low, high = waves[wave]
-        return pltpu.make_async_remote_copy(
-            src_ref=recv1.at[pl.ds(low, high - low), at_outer(r)],
-            dst_ref=recv2.at[o, pl.ds(low, high - low)],
-            send_sem=z_send.at[wave, r], recv_sem=z_recv.at[wave, outer_n - r],
-            device_id={"outer": at_outer(r)}, device_id_type=MESH,
-        )
-
-    def z_arrival(wave, r):
-        low, high = waves[wave]
-        here = recv2.at[at_outer(r), pl.ds(low, high - low)]
-        return pltpu.make_async_remote_copy(
-            src_ref=here, dst_ref=here,
-            send_sem=z_send.at[wave, r], recv_sem=z_recv.at[wave, r],
-            device_id={"outer": at_outer(r)}, device_id_type=MESH,
-        )
+        d_start(slot, 1)
+    recv2[o, 0] = send1[0, o]
 
     def q_copy(d):
         return pltpu.make_async_remote_copy(
@@ -176,89 +185,69 @@
             device_id={"inner": at_inner(d)}, device_id_type=MESH,
         )
 
-    def z_start(wave):
-        def start(r, carry):
-            z_copy(wave, r).start()
-            return carry
-
-        lax.fori_loop(1, outer_n, start, 0)
-
-    z_start(0)
-
-    for load in loads[3:]:
+    for load in loads[4:]:
         load.wait()
-    for n in range(w_rows.shape[0]):
-        span = pl.ds(n * w_rows.shape[2], w_rows.shape[2])
-        w_rows[n] = w_buf[:, span].astype(F32)
+    mine = pl.ds(core * (parts // 2), parts // 2)
+    spans = w_rows.shape[0]
+
+    def span_of(n):
+        return pl.ds(n * w_rows.shape[2], w_rows.shape[2])
+
+    def w_copy(d, n):
+        held = weights.at[c, mine, span_of(n)]
+        return pltpu.make_async_remote_copy(
+            src_ref=held, dst_ref=held, send_sem=w_send.at[d, n], recv_sem=w_recv.at[chan_n - d, n],
+            device_id={"chan": at_chan(d)}, device_id_type=MESH,
+        )
+
+    def f_copy(d, half):
+        held = weights.at[at_chan(d), pl.ds(half * (parts // 2), parts // 2)]
+        return pltpu.make_async_remote_copy(
+            src_ref=held, dst_ref=held, send_sem=f_send.at[d], recv_sem=f_recv.at[d],
+            device_id={"outer": sibling}, device_id_type=MESH,
+        )
+
+    def w_part(n):
+        w_rows[n] = w_buf[:, span_of(n)].astype(F32)
         for cc in range(per):
             rows = w_rows[n, pl.ds(cc, slabs, stride=per), :]
-            weights[c, cc // each, span, pl.ds(cc % each * slabs, slabs)] = rows.T.astype(BF16)
-    mine = pl.ds(core * (parts // 2), parts // 2)
-
-    def w_copy(d):
-        held = weights.at[c, mine]
-        return pltpu.make_async_remote_copy(
-            src_ref=held, dst_ref=held, send_sem=w_send.at[d], recv_sem=w_recv.at[chan_n - d],
-            device_id={"chan": at_chan(d)}, device_id_type=MESH,
-        )
-
-    def f_copy(d, half):
-        held = weights.at[at_chan(d), pl.ds(half * (parts // 2), parts // 2)]
-        return pltpu.make_async_remote_copy(
-            src_ref=held, dst_ref=held, send_sem=f_send.at[d], recv_sem=f_recv.at[d],
-            device_id={"outer": sibling}, device_id_type=MESH,
-        )
-
-    for d in range(1, chan_n):
-        w_copy(d).start()
-
-    gain = jnp.broadcast_to(skip_ref[:, cols(i)], (tok, block)).T
-
-    def keep_product(slot):
-        both = recv1[slot].astype(F32)
-        rows = pl.ds(slot * block, block)
-        folded_p[rows, :] = both[:, :per].reshape(block, tok) * gain
+            weights[c, cc // each, span_of(n), pl.ds(cc % each * slabs, slabs)] = rows.T.astype(BF16)
+        for d in range(1, chan_n):
+            w_copy(d, n).start()
+
+    for n in range(spans):
+        w_part(n)
+    gains[...] = jnp.broadcast_to(skip_ref[:, cols(i)], (tok, block)).T
+
+    def q_start():
+        for d in order[1:]:
+            q_copy(d).start()
+
+    for slot in range(inner_n):
+        if slot == Q_AT:
+            q_start()
+        d_all(slot).wait_recv()
         place = at_inner(order[slot])
-        for cc in range(per):
-            gate_p[cc, place] = folded_p[pl.ds(slot * block + cc, outer_n, stride=per), :]
-
-    for wave, (low, high) in enumerate(waves):
-        if wave > 0:
-            for slot in range(low, high):
-                y_copy(slot, (inner_n - order[slot]) % inner_n).wait_recv()
-            z_start(wave)
-        for slot in range(low, high):
-            keep_product(slot)
-    for d in order[1:]:
-        q_copy(d).start()
-
-    for wave, (low, high) in enumerate(waves):
-
-        def z_wait(r, carry, wave=wave):
-            z_arrival(wave, r).wait_recv()
-            return carry
-
-        lax.fori_loop(1, outer_n, z_wait, 0)
-        for slot in range(low, high):
-            recv2[o, slot] = recv1[slot, o]
-        for slot in range(low, high):
-            place = at_inner(order[slot])
-            for source in range(outer_n):
-                row = pl.multiple_of((source * inner_n + place) * (2 * per), 2 * per)
-                signals[pl.ds(row, 2 * per), :] = recv2[source, slot].astype(F32)
+        for source in range(outer_n):
+            row = pl.multiple_of((source * inner_n + place) * (2 * per), 2 * per)
+            signals[pl.ds(row, 2 * per), :] = recv2[source, slot].astype(F32)
+    if Q_AT >= inner_n:
+        q_start()
 
     padded = twist_ref.shape[1]
     cos_twist, sin_twist = twist_ref[0], twist_ref[1]
+    own_gains = gains[pl.ds(pl.multiple_of(o * per, per), per), :]
 
     def wide(table, times):
         return jnp.concatenate([table] * times, axis=1)
 
     def convolve(first):
-        both = []
-        for channel in (first, first + 1):
-            for kind in range(2):
-                both.append(signals[pl.ds(channel + kind * per, slabs, stride=2 * per), :].astype(BF16))
-        x = jnp.concatenate(both, axis=1)
+        both = [
+            signals[pl.ds(channel + kind * per, slabs, stride=2 * per), :]
+            for channel in (first, first + 1)
+            for kind in range(2)
+        ]
+        x = jnp.concatenate([b.astype(BF16) for b in both], axis=1)
         y = dot(section_ref[...], jnp.concatenate([x, x], axis=0))
         real, imag = y[:padded], y[padded:]
         cos4, sin4 = wide(cos_twist, 4), wide(sin_twist, 4)
@@ -288,8 +277,10 @@
             )
         high, low = halves(jnp.concatenate(ups, axis=1))
         conv = dot(back_ref[0], high) + (dot(back_ref[1], high) + dot(back_ref[0], low))
-        conv = [conv[:, n * tok : (n + 1) * tok].reshape(outer_n, inner_n, tok) for n in range(2)]
-        return jnp.concatenate(conv, axis=1).astype(BF16)
+        mixed = [
+            conv[:, n * tok : (n + 1) * tok] + own_gains[first + n : first + n + 1] * both[2 * n] for n in range(2)
+        ]
+        return jnp.concatenate([m.reshape(outer_n, inner_n, tok) for m in mixed], axis=1).astype(BF16)
 
     def part_rows(h):
         return pl.ds(h * each * inner_n, each * inner_n)
@@ -322,9 +313,9 @@
     for d in range(1, inner_n):
         q_copy(inner_n - d).wait_recv()
     for slab in range(inner_n):
-        folded_q[pl.ds(slab * block, block), :] = q_recv[slab].astype(F32).T
+        folded[pl.ds(slab * block, block), :] = q_recv[slab].astype(F32).T
         for cc in range(per):
-            gate_q[cc, slab] = folded_q[pl.ds(slab * block + cc, outer_n, stride=per), :]
+            gate_q[cc, slab] = folded[pl.ds(slab * block + cc, outer_n, stride=per), :]
 
     def x_copy(h, d):
         return pltpu.make_async_remote_copy(
@@ -348,16 +339,12 @@
             cc = h * each + e
             for slab in range(inner_n):
                 conv = conv_rows[pl.ds(first + e * inner_n + slab, outer_n, stride=count), :]
-                value = (gate_q[cc, slab] * (conv + gate_p[cc, slab])).astype(BF16)
+                value = (gate_q[cc, slab] * conv).astype(BF16)
                 gx[h, slab // near, e, :, pl.ds(slab % near * tok, tok)] = value
         for d in range(1, chan_n):
             x_copy(h, d).start()
         gated[h, c, :, i] = gx[h, c]
 
-    for d in range(1, chan_n):
-        w_copy(chan_n - d).wait_recv()
-        f_copy(d, core).start()
-
     longest = inner_n // 2
 
     def reach(way, h):
@@ -377,7 +364,12 @@
     for h in range(parts):
         for r in range(1, longest + 2):
             events.append((RING_LAG * h + r, h, r))
-    for _, h, r in sorted(events):
+    for count, (_, h, r) in enumerate(sorted(events)):
+        if count == PASS_AT:
+            for d in range(1, chan_n):
+                for n in range(spans):
+                    w_copy(chan_n - d, n).wait_recv()
+                f_copy(d, core).start()
         if r == 1:
             for d in range(1, chan_n):
                 x_copy(h, chan_n - d).wait_recv()
@@ -400,21 +392,20 @@
             else:
                 out_ref[...] = (total[...] + part).T.astype(BF16)
 
-    for slot in range(1, inner_n):
-        y_copy(slot, order[slot]).wait_send()
+    for slot in range(inner_n):
+        d_all(slot).wait_send()
     for d in range(1, inner_n):
         q_copy(d).wait_send()
 
     def sent(r, carry):
-        for wave in range(len(waves)):
-            z_copy(wave, r).wait_send()
         for h in range(parts):
             b_copy(h, r).wait_send()
         return carry
 
     lax.fori_loop(1, outer_n, sent, 0)
     for d in range(1, chan_n):
-        w_copy(d).wait_send()
+        for n in range(spans):
+            w_copy(d, n).wait_send()
         f_copy(d, core).wait_send()
         for h in range(parts):
             x_copy(h, d).wait_send()
@@ -433,18 +424,18 @@
     width = out_weight.shape[1]
     coarse = inner_n * tok
     piece = coarse // chan_n
-    held = tables(slabs, tok)
+    held = (*tables(slabs, tok), pick_table(outer_n, per))
     parts = PARTS
     each = per // parts
     lanes = min(width, 128)
     sizes = (outer_n, inner_n, chan_n, tok, per, parts)
-    waves = max(2, inner_n // 2)
+    spans = width // lanes
     dma = pltpu.SemaphoreType.DMA
     hbm = pl.BlockSpec(memory_space=pltpu.HBM)
     return pl.pallas_call(
         functools.partial(kernel, sizes),
         out_shape=jax.ShapeDtypeStruct((piece, width), BF16),
-        in_specs=[hbm] * 11,
+        in_specs=[hbm] * 12,
         out_specs=pl.BlockSpec(memory_space=pltpu.VMEM),
         scratch_shapes=[
             pltpu.VMEM((tok, chans), BF16),
@@ -454,37 +445,34 @@
             pltpu.VMEM((chans, width), BF16),
             *(pltpu.VMEM(t.shape, t.dtype) for t in held),
             pltpu.VMEM((inner_n, outer_n, 2 * per, tok), BF16),
-            pltpu.VMEM((inner_n, outer_n, 2 * per, tok), BF16),
             pltpu.VMEM((outer_n, inner_n, 2 * per, tok), BF16),
             pltpu.VMEM((slabs * 2 * per, tok), F32),
             pltpu.VMEM((outer_n, per * inner_n, tok), BF16),
             pltpu.VMEM((outer_n, per * inner_n, tok), BF16),
             pltpu.VMEM((outer_n * per * inner_n, tok), F32),
             pltpu.VMEM((inner_n, tok, block), BF16),
+            pltpu.VMEM((block, tok), F32),
             pltpu.VMEM((inner_n * block, tok), F32),
-            pltpu.VMEM((inner_n * block, tok), F32),
-            pltpu.VMEM((per, inner_n, outer_n, tok), F32),
             pltpu.VMEM((per, inner_n, outer_n, tok), F32),
             pltpu.VMEM((parts, chan_n, each, outer_n, piece), BF16),
             pltpu.VMEM((parts, chan_n, each, inner_n, outer_n, piece), BF16),
             pltpu.VMEM((width // lanes, chans, lanes), F32),
             pltpu.VMEM((chan_n, parts, width, each * slabs), BF16),
             pltpu.VMEM((width, piece), F32),
-            dma((11,)),
+            dma((12,)),
+            pltpu.SemaphoreType.REGULAR,
             dma((inner_n,)),
             dma((inner_n,)),
             dma((inner_n,)),
             dma((inner_n,)),
-            dma((waves, outer_n)),
-            dma((waves, outer_n)),
             dma((parts, outer_n)),
             dma((parts, outer_n)),
             dma((parts, chan_n)),
             dma((parts, chan_n)),
             dma((2, parts, inner_n // 2)),
             dma((2, parts, inner_n // 2)),
-            dma((chan_n,)),
-            dma((chan_n,)),
+            dma((chan_n, spans)),
+            dma((chan_n, spans)),
             dma((chan_n,)),
             dma((chan_n,)),
         ],

time: 78.2 us -> 73.5 us (0.940)
  the two profiles are of different devices: /device:TPU:20 before, /device:TPU:1 now
where the time goes in v3:
time: 73.5 us; the launch traced here: 72.7 us
  Pallas kernels  71 us (97%)
  local copies, waits for them, and re-layouts  1.67 us (2%)
    pallas_call x1, Pallas kernels, local(): pl.pallas_call(functools.partial(kernel, sizes), out_shape=jax.ShapeDtype...  71 us
    unnamed x1, local copies, waits for them, and re-layouts  1.67 us

profile of v3, /device:TPU:1, one launch (start us, length us, event | category | flops | bytes accessed | tf_op | source)
XLA Modules:
  0.0 72.7 jit_solution(3230613897313801997)
XLA Ops:
  0.0 71.0 %shard_map.118 = bf16[256,512]{1,0:T(8,128)(2,1)} custom-call(bf16[128,1024]{1,0:T(8,128)(2,1)} %q_hbm.1, bf16[128,1024]{1,0:T(8,128)(2,1)} %k_hbm.1, bf16[128,1024]{1,0:T(8,128)(2,1)} %v_hbm.1, bf16[128,1024]{1,0:T(8,128)(2,1)} %taps_hbm.1, f32[1,1024]{1,0:T(1,128)} %bitcast.1, bf16[1024,512]{1,0:T(8,128)(2,1)} %w_hbm.1, ...), custom_call_target="tpu_custom_call" | custom-call | tf_op jit(solution)/shard_map/pallas_call | solution.py:435
  71.0 1.7 %copy.14 = bf16[256,512]{1,0:T(8,128)(2,1)} copy(bf16[256,512]{1,0:T(8,128)(2,1)} %shard_map.118) | data formatting | bytes 524288

commit v4 on v3

--- a/solution.py
+++ b/solution.py
@@ -13,7 +13,7 @@
 BF16 = jnp.bfloat16
 PARTS = 4
 RING_LAG = 0.3
-Q_AT = 4
+Q_AT = 1
 PASS_AT = 3
 
 
@@ -81,9 +81,9 @@
     section_hbm, twist_hbm, forth_hbm, inverse_hbm, back_hbm, pick_hbm,
     out_ref,
     k_buf, v_buf, taps_buf, skip_ref, w_buf, section_ref, twist_ref, forth_ref, inverse_ref, back_ref, pick_ref,
-    send1, recv2, signals, send2, recv3, conv_rows, q_recv, gains, folded, gate_q,
+    send1, recv1, recv2, signals, send2, recv3, conv_rows, q_recv, gains, folded, gate_q,
     gx, gated, w_rows, weights, total,
-    load_sem, ready, d_send, d_recv, q_send, q_recv_sem, b_send, b_recv, x_send, x_recv,
+    load_sem, ready, y_send, y_recv, z_send, z_recv, d_send, d_recv, q_send, q_recv_sem, b_send, b_recv, x_send, x_recv,
     g_send, g_recv, w_send, w_recv, f_send, f_recv,
 ):
     outer_n, inner_n, chan_n, tok, per, parts = sizes
@@ -93,6 +93,8 @@
     o, i, c = lax.axis_index("outer"), lax.axis_index("inner"), lax.axis_index("chan")
     order = near_first(inner_n)
     near = inner_n // chan_n
+    passed = inner_n // 2
+    waves = [(low, low + 2) for low in range(1, passed + 1, 2)]
     core = lax.rem(o, 2)
     sibling = o + 1 - 2 * core
 
@@ -160,6 +162,30 @@
             device_id={"outer": sibling}, device_id_type=MESH,
         )
 
+    def y_copy(slot, d):
+        there = order.index((inner_n - d) % inner_n)
+        return pltpu.make_async_remote_copy(
+            src_ref=send1.at[slot], dst_ref=recv1.at[there - 1], send_sem=y_send.at[slot], recv_sem=y_recv.at[there],
+            device_id={"inner": at_inner(d)}, device_id_type=MESH,
+        )
+
+    def z_copy(wave, r):
+        low, high = waves[wave]
+        return pltpu.make_async_remote_copy(
+            src_ref=recv1.at[pl.ds(low - 1, high - low), at_outer(r)],
+            dst_ref=recv2.at[o, pl.ds(low, high - low)],
+            send_sem=z_send.at[wave], recv_sem=z_recv.at[wave],
+            device_id={"outer": at_outer(r)}, device_id_type=MESH,
+        )
+
+    def z_all(wave):
+        low, high = waves[wave]
+        held = recv2.at[pl.ds(0, outer_n - 1), pl.ds(low, high - low)]
+        return pltpu.make_async_remote_copy(
+            src_ref=held, dst_ref=held, send_sem=z_send.at[wave], recv_sem=z_recv.at[wave],
+            device_id={"outer": sibling}, device_id_type=MESH,
+        )
+
     def d_start(slot, first):
         def start(r, carry):
             d_copy(slot, r).start()
@@ -167,17 +193,6 @@
 
         lax.fori_loop(first, outer_n, start, 0)
 
-    for slot in range(inner_n):
-        send1[slot] = pack(at_inner(order[slot]))
-        if slot == 0:
-            d_start(0, 1)
-        else:
-            d_copy(slot, 0).start()
-    pl.semaphore_wait(ready, outer_n - 1)
-    for slot in range(1, inner_n):
-        d_start(slot, 1)
-    recv2[o, 0] = send1[0, o]
-
     def q_copy(d):
         return pltpu.make_async_remote_copy(
             src_ref=q_hbm.at[:, cols(at_inner(d))], dst_ref=q_recv.at[i],
@@ -185,6 +200,18 @@
             device_id={"inner": at_inner(d)}, device_id_type=MESH,
         )
 
+    def q_start():
+        for d in order[1:]:
+            q_copy(d).start()
+
+    for slot in range(1, passed + 1):
+        send1[slot] = pack(at_inner(order[slot]))
+        y_copy(slot, order[slot]).start()
+    send1[0] = pack(i)
+    d_start(0, 1)
+    recv2[o, 0] = send1[0, o]
+    for slot in range(passed + 1, inner_n):
+        send1[slot] = pack(at_inner(order[slot]))
     for load in loads[4:]:
         load.wait()
     mine = pl.ds(core * (parts // 2), parts // 2)
@@ -194,14 +221,14 @@
         return pl.ds(n * w_rows.shape[2], w_rows.shape[2])
 
     def w_copy(d, n):
-        held = weights.at[c, mine, span_of(n)]
-        return pltpu.make_async_remote_copy(
-            src_ref=held, dst_ref=held, send_sem=w_send.at[d, n], recv_sem=w_recv.at[chan_n - d, n],
+        return pltpu.make_async_remote_copy(
+            src_ref=weights.at[0, mine, span_of(n)], dst_ref=weights.at[chan_n - d, mine, span_of(n)],
+            send_sem=w_send.at[d, n], recv_sem=w_recv.at[chan_n - d, n],
             device_id={"chan": at_chan(d)}, device_id_type=MESH,
         )
 
     def f_copy(d, half):
-        held = weights.at[at_chan(d), pl.ds(half * (parts // 2), parts // 2)]
+        held = weights.at[d, pl.ds(half * (parts // 2), parts // 2)]
         return pltpu.make_async_remote_copy(
             src_ref=held, dst_ref=held, send_sem=f_send.at[d], recv_sem=f_recv.at[d],
             device_id={"outer": sibling}, device_id_type=MESH,
@@ -211,7 +238,7 @@
         w_rows[n] = w_buf[:, span_of(n)].astype(F32)
         for cc in range(per):
             rows = w_rows[n, pl.ds(cc, slabs, stride=per), :]
-            weights[c, cc // each, span_of(n), pl.ds(cc % each * slabs, slabs)] = rows.T.astype(BF16)
+            weights[0, cc // each, span_of(n), pl.ds(cc % each * slabs, slabs)] = rows.T.astype(BF16)
         for d in range(1, chan_n):
             w_copy(d, n).start()
 
@@ -219,20 +246,40 @@
         w_part(n)
     gains[...] = jnp.broadcast_to(skip_ref[:, cols(i)], (tok, block)).T
 
-    def q_start():
-        for d in order[1:]:
-            q_copy(d).start()
-
-    for slot in range(inner_n):
-        if slot == Q_AT:
-            q_start()
-        d_all(slot).wait_recv()
+    if Q_AT == 0:
+        q_start()
+    pl.semaphore_wait(ready, outer_n - 1)
+    for slot in range(passed + 1, inner_n):
+        d_start(slot, 0)
+
+    for wave, (low, high) in enumerate(waves):
+        for slot in range(low, high):
+            y_copy(slot, (inner_n - order[slot]) % inner_n).wait_recv()
+
+        def z_start(r, carry, wave=wave):
+            z_copy(wave, r).start()
+            return carry
+
+        lax.fori_loop(1, outer_n, z_start, 0)
+        for slot in range(low, high):
+            recv2[o, slot] = recv1[slot - 1, o]
+    if Q_AT == 1:
+        q_start()
+    def spread(slot):
         place = at_inner(order[slot])
         for source in range(outer_n):
             row = pl.multiple_of((source * inner_n + place) * (2 * per), 2 * per)
             signals[pl.ds(row, 2 * per), :] = recv2[source, slot].astype(F32)
-    if Q_AT >= inner_n:
+
+    for slot in [0, *range(passed + 1, inner_n)]:
+        d_all(slot).wait_recv()
+        spread(slot)
+    if Q_AT == 2:
         q_start()
+    for wave, (low, high) in enumerate(waves):
+        z_all(wave).wait_recv()
+        for slot in range(low, high):
+            spread(slot)
 
     padded = twist_ref.shape[1]
     cos_twist, sin_twist = twist_ref[0], twist_ref[1]
@@ -319,9 +366,27 @@
 
     def x_copy(h, d):
         return pltpu.make_async_remote_copy(
-            src_ref=gx.at[h, at_chan(d)], dst_ref=gated.at[h, c, :, i],
+            src_ref=gx.at[h, at_chan(d)], dst_ref=gated.at[h, chan_n - d, :, i],
             send_sem=x_send.at[h, d], recv_sem=x_recv.at[h, chan_n - d],
             device_id={"chan": at_chan(d)}, device_id_type=MESH,
+        )
+
+    longest = inner_n // 2
+    OWN, REST, WHOLE = 0, 1, 2
+
+    def reach(way, h):
+        return longest if (h + way) % 2 == 0 else inner_n - 1 - longest
+
+    def g_copy(way, h, r, which, arrival=False):
+        step = 1 if way == 0 else inner_n - 1
+        source = at_inner((inner_n - step) * (r if arrival else r - 1) % inner_n)
+        groups = (pl.ds(0, 1), pl.ds(1, chan_n - 1), pl.ds(0, chan_n))[which]
+        held = gated.at[h, groups, :, source]
+        place = 0 if which == OWN else r
+        return pltpu.make_async_remote_copy(
+            src_ref=held, dst_ref=held,
+            send_sem=g_send.at[way, h, place], recv_sem=g_recv.at[way, h, place],
+            device_id={"inner": at_inner(step)}, device_id_type=MESH,
         )
 
     for h in range(parts):
@@ -343,22 +408,9 @@
                 gx[h, slab // near, e, :, pl.ds(slab % near * tok, tok)] = value
         for d in range(1, chan_n):
             x_copy(h, d).start()
-        gated[h, c, :, i] = gx[h, c]
-
-    longest = inner_n // 2
-
-    def reach(way, h):
-        return longest if (h + way) % 2 == 0 else inner_n - 1 - longest
-
-    def g_copy(way, h, r, arrival=False):
-        step = 1 if way == 0 else inner_n - 1
-        source = at_inner((inner_n - step) * (r if arrival else r - 1) % inner_n)
-        held = gated.at[h, :, :, source]
-        return pltpu.make_async_remote_copy(
-            src_ref=held, dst_ref=held,
-            send_sem=g_send.at[way, h, r - 1], recv_sem=g_recv.at[way, h, r - 1],
-            device_id={"inner": at_inner(step)}, device_id_type=MESH,
-        )
+        gated[h, 0, :, i] = gx[h, c]
+        for way in range(2):
+            g_copy(way, h, 1, OWN).start()
 
     events = []
     for h in range(parts):
@@ -374,10 +426,12 @@
             for d in range(1, chan_n):
                 x_copy(h, chan_n - d).wait_recv()
         for way in range(2):
+            if r == 2:
+                g_copy(way, h, 1, OWN, arrival=True).wait_recv()
             if 1 < r <= reach(way, h) + 1:
-                g_copy(way, h, r - 1, arrival=True).wait_recv()
+                g_copy(way, h, r - 1, REST if r == 2 else WHOLE, arrival=True).wait_recv()
             if r <= reach(way, h):
-                g_copy(way, h, r).start()
+                g_copy(way, h, r, REST if r == 1 else WHOLE).start()
         if r == longest + 1:
             if h == 0:
                 for d in range(1, chan_n):
@@ -392,8 +446,12 @@
             else:
                 out_ref[...] = (total[...] + part).T.astype(BF16)
 
-    for slot in range(inner_n):
+    for slot in [0, *range(passed + 1, inner_n)]:
         d_all(slot).wait_send()
+    for slot in range(1, passed + 1):
+        y_copy(slot, order[slot]).wait_send()
+    for wave in range(len(waves)):
+        z_all(wave).wait_send()
     for d in range(1, inner_n):
         q_copy(d).wait_send()
 
@@ -411,8 +469,9 @@
             x_copy(h, d).wait_send()
     for h in range(parts):
         for way in range(2):
+            g_copy(way, h, 1, OWN).wait_send()
             for r in range(1, reach(way, h) + 1):
-                g_copy(way, h, r).wait_send()
+                g_copy(way, h, r, REST if r == 1 else WHOLE).wait_send()
 
 
 def local(q_stream, k_stream, v_stream, filter_taps, skip_gain, out_weight):
@@ -445,6 +504,7 @@
             pltpu.VMEM((chans, width), BF16),
             *(pltpu.VMEM(t.shape, t.dtype) for t in held),
             pltpu.VMEM((inner_n, outer_n, 2 * per, tok), BF16),
+            pltpu.VMEM((inner_n // 2, outer_n, 2 * per, tok), BF16),
             pltpu.VMEM((outer_n, inner_n, 2 * per, tok), BF16),
             pltpu.VMEM((slabs * 2 * per, tok), F32),
             pltpu.VMEM((outer_n, per * inner_n, tok), BF16),
@@ -463,14 +523,18 @@
             pltpu.SemaphoreType.REGULAR,
             dma((inner_n,)),
             dma((inner_n,)),
+            dma((inner_n // 4,)),
+            dma((inner_n // 4,)),
+            dma((inner_n,)),
+            dma((inner_n,)),
             dma((inner_n,)),
             dma((inner_n,)),
             dma((parts, outer_n)),
             dma((parts, outer_n)),
             dma((parts, chan_n)),
             dma((parts, chan_n)),
-            dma((2, parts, inner_n // 2)),
-            dma((2, parts, inner_n // 2)),
+            dma((2, parts, inner_n // 2 + 1)),
+            dma((2, parts, inner_n // 2 + 1)),
             dma((chan_n, spans)),
             dma((chan_n, spans)),
             dma((chan_n,)),

time: 73.5 us -> 71.5 us (0.973)
  Pallas kernels: 71 us -> 69.1 us
    pallas_call x1, Pallas kernels: 71 us -> 69.1 us  [local(): pl.pallas_call(functools.partial(kernel, sizes), out_shape=jax.ShapeDtype...]
where the time goes in v4:
time: 71.5 us; the launch traced here: 70.8 us
  Pallas kernels  69.1 us (97%)
  local copies, waits for them, and re-layouts  1.67 us (2%)
    pallas_call x1, Pallas kernels, local(): pl.pallas_call(functools.partial(kernel, sizes), out_shape=jax.ShapeDtype...  69.1 us
    unnamed x1, local copies, waits for them, and re-layouts  1.67 us

profile of v4, /device:TPU:1, one launch (start us, length us, event | category | flops | bytes accessed | tf_op | source)
XLA Modules:
  0.0 70.8 jit_solution(693730283029243985)
XLA Ops:
  0.0 69.1 %shard_map.118 = bf16[256,512]{1,0:T(8,128)(2,1)} custom-call(bf16[128,1024]{1,0:T(8,128)(2,1)} %q_hbm.1, bf16[128,1024]{1,0:T(8,128)(2,1)} %k_hbm.1, bf16[128,1024]{1,0:T(8,128)(2,1)} %v_hbm.1, bf16[128,1024]{1,0:T(8,128)(2,1)} %taps_hbm.1, f32[1,1024]{1,0:T(1,128)} %bitcast.1, bf16[1024,512]{1,0:T(8,128)(2,1)} %w_hbm.1, ...), custom_call_target="tpu_custom_call" | custom-call | tf_op jit(solution)/shard_map/pallas_call | solution.py:494
  69.1 1.7 %copy.14 = bf16[256,512]{1,0:T(8,128)(2,1)} copy(bf16[256,512]{1,0:T(8,128)(2,1)} %shard_map.118) | data formatting | bytes 524288

commit v5 on v4

--- a/solution.py
+++ b/solution.py
@@ -13,7 +13,6 @@
 BF16 = jnp.bfloat16
 PARTS = 4
 RING_LAG = 0.3
-Q_AT = 1
 PASS_AT = 3
 
 
@@ -68,11 +67,11 @@
     return dot(high, table[0]) + (dot(high, table[1]) + dot(low, table[0]))
 
 
-def near_first(n):
+def path_order(n):
     order = [0]
-    for d in range(1, n // 2):
+    for d in range(1, n // 2 - 1):
         order += [d, n - d]
-    return order + [n // 2]
+    return order + [n // 2, n // 2 - 1, n // 2 + 1]
 
 
 def kernel(
@@ -81,9 +80,9 @@
     section_hbm, twist_hbm, forth_hbm, inverse_hbm, back_hbm, pick_hbm,
     out_ref,
     k_buf, v_buf, taps_buf, skip_ref, w_buf, section_ref, twist_ref, forth_ref, inverse_ref, back_ref, pick_ref,
-    send1, recv1, recv2, signals, send2, recv3, conv_rows, q_recv, gains, folded, gate_q,
+    send1, recv1, middle, recv2, signals, send2, recv3, conv_rows, q_recv, gains, folded, gate_q,
     gx, gated, w_rows, weights, total,
-    load_sem, ready, y_send, y_recv, z_send, z_recv, d_send, d_recv, q_send, q_recv_sem, b_send, b_recv, x_send, x_recv,
+    load_sem, y_send, y_recv, z_send, z_recv, t_send, t_recv, d_send, d_recv, q_send, q_recv_sem, b_send, b_recv, x_send, x_recv,
     g_send, g_recv, w_send, w_recv, f_send, f_recv,
 ):
     outer_n, inner_n, chan_n, tok, per, parts = sizes
@@ -91,10 +90,11 @@
     block = outer_n * per
     each = per // parts
     o, i, c = lax.axis_index("outer"), lax.axis_index("inner"), lax.axis_index("chan")
-    order = near_first(inner_n)
+    order = path_order(inner_n)
     near = inner_n // chan_n
-    passed = inner_n // 2
-    waves = [(low, low + 2) for low in range(1, passed + 1, 2)]
+    passed = inner_n - 3
+    waves = [(low, min(low + 2, passed + 1)) for low in range(1, passed + 1, 2)]
+    turned = (passed + 1, passed + 2)
     core = lax.rem(o, 2)
     sibling = o + 1 - 2 * core
 
@@ -135,8 +135,6 @@
     for load in loads:
         load.start()
     pl.semaphore_wait(barrier, inner_n + outer_n + chan_n - 3)
-    for r in range(1, outer_n):
-        pl.semaphore_signal(ready, inc=1, device_id={"outer": at_outer(r)}, device_id_type=MESH)
     for load in loads[:4]:
         load.wait()
 
@@ -147,19 +145,39 @@
         rows = lax.dot_general(pick_ref[...], both, (((1,), (1,)), ((), ())), preferred_element_type=F32)
         return rows.reshape(outer_n, 2 * per, tok).astype(BF16)
 
-    def d_copy(slot, r):
-        there = order.index((inner_n - order[slot]) % inner_n)
-        return pltpu.make_async_remote_copy(
-            src_ref=send1.at[slot, at_outer(r)], dst_ref=recv2.at[o, there],
+    def d_copy(r):
+        return pltpu.make_async_remote_copy(
+            src_ref=send1.at[0, at_outer(r)], dst_ref=recv2.at[o, 0], send_sem=d_send.at[0], recv_sem=d_recv.at[0],
+            device_id={"outer": at_outer(r)}, device_id_type=MESH,
+        )
+
+    def d_all():
+        held = recv2.at[pl.ds(0, outer_n - 1), 0]
+        return pltpu.make_async_remote_copy(
+            src_ref=held, dst_ref=held, send_sem=d_send.at[0], recv_sem=d_recv.at[0],
+            device_id={"outer": sibling}, device_id_type=MESH,
+        )
+
+    def t_copy(r):
+        return pltpu.make_async_remote_copy(
+            src_ref=send1.at[pl.ds(turned[0], 2), at_outer(r)], dst_ref=middle.at[:, o],
+            send_sem=t_send.at[0], recv_sem=t_recv.at[0],
+            device_id={"outer": at_outer(r)}, device_id_type=MESH,
+        )
+
+    def t_all():
+        held = middle.at[:, pl.ds(0, outer_n - 1)]
+        return pltpu.make_async_remote_copy(
+            src_ref=held, dst_ref=held, send_sem=t_send.at[0], recv_sem=t_recv.at[0],
+            device_id={"outer": sibling}, device_id_type=MESH,
+        )
+
+    def turn_copy(slot, d):
+        there = order.index((inner_n - d) % inner_n)
+        return pltpu.make_async_remote_copy(
+            src_ref=middle.at[slot - turned[0]], dst_ref=recv2.at[:, there],
             send_sem=d_send.at[slot], recv_sem=d_recv.at[there],
-            device_id={"outer": at_outer(r), "inner": at_inner(order[slot])}, device_id_type=MESH,
-        )
-
-    def d_all(slot):
-        held = recv2.at[pl.ds(0, outer_n - 1 if slot == 0 else outer_n), slot]
-        return pltpu.make_async_remote_copy(
-            src_ref=held, dst_ref=held, send_sem=d_send.at[slot], recv_sem=d_recv.at[slot],
-            device_id={"outer": sibling}, device_id_type=MESH,
+            device_id={"inner": at_inner(d)}, device_id_type=MESH,
         )
 
     def y_copy(slot, d):
@@ -186,13 +204,6 @@
             device_id={"outer": sibling}, device_id_type=MESH,
         )
 
-    def d_start(slot, first):
-        def start(r, carry):
-            d_copy(slot, r).start()
-            return carry
-
-        lax.fori_loop(first, outer_n, start, 0)
-
     def q_copy(d):
         return pltpu.make_async_remote_copy(
             src_ref=q_hbm.at[:, cols(at_inner(d))], dst_ref=q_recv.at[i],
@@ -204,14 +215,30 @@
         for d in order[1:]:
             q_copy(d).start()
 
-    for slot in range(1, passed + 1):
+    def y_go(slot):
         send1[slot] = pack(at_inner(order[slot]))
         y_copy(slot, order[slot]).start()
+
+    for slot in range(1, passed):
+        y_go(slot)
+    for slot in turned:
+        send1[slot] = pack(at_inner(order[slot]))
+
+    def t_start(r, carry):
+        t_copy(r).start()
+        return carry
+
+    def d_start(r, carry):
+        d_copy(r).start()
+        return carry
+
+    lax.fori_loop(1, outer_n, t_start, 0)
+    middle[:, o] = send1[turned[0] : turned[1] + 1, o]
     send1[0] = pack(i)
-    d_start(0, 1)
+    lax.fori_loop(1, outer_n, d_start, 0)
     recv2[o, 0] = send1[0, o]
-    for slot in range(passed + 1, inner_n):
-        send1[slot] = pack(at_inner(order[slot]))
+    y_go(passed)
+
     for load in loads[4:]:
         load.wait()
     mine = pl.ds(core * (parts // 2), parts // 2)
@@ -246,12 +273,6 @@
         w_part(n)
     gains[...] = jnp.broadcast_to(skip_ref[:, cols(i)], (tok, block)).T
 
-    if Q_AT == 0:
-        q_start()
-    pl.semaphore_wait(ready, outer_n - 1)
-    for slot in range(passed + 1, inner_n):
-        d_start(slot, 0)
-
     for wave, (low, high) in enumerate(waves):
         for slot in range(low, high):
             y_copy(slot, (inner_n - order[slot]) % inner_n).wait_recv()
@@ -263,24 +284,26 @@
         lax.fori_loop(1, outer_n, z_start, 0)
         for slot in range(low, high):
             recv2[o, slot] = recv1[slot - 1, o]
-    if Q_AT == 1:
-        q_start()
+    t_all().wait_recv()
+    for slot in turned:
+        turn_copy(slot, order[slot]).start()
     def spread(slot):
         place = at_inner(order[slot])
         for source in range(outer_n):
             row = pl.multiple_of((source * inner_n + place) * (2 * per), 2 * per)
             signals[pl.ds(row, 2 * per), :] = recv2[source, slot].astype(F32)
 
-    for slot in [0, *range(passed + 1, inner_n)]:
-        d_all(slot).wait_recv()
-        spread(slot)
-    if Q_AT == 2:
-        q_start()
+    d_all().wait_recv()
+    spread(0)
     for wave, (low, high) in enumerate(waves):
         z_all(wave).wait_recv()
         for slot in range(low, high):
             spread(slot)
-
+    for slot in turned:
+        turn_copy(slot, inner_n - order[slot]).wait_recv()
+        spread(slot)
+
+    q_start()
     padded = twist_ref.shape[1]
     cos_twist, sin_twist = twist_ref[0], twist_ref[1]
     own_gains = gains[pl.ds(pl.multiple_of(o * per, per), per), :]
@@ -446,8 +469,10 @@
             else:
                 out_ref[...] = (total[...] + part).T.astype(BF16)
 
-    for slot in [0, *range(passed + 1, inner_n)]:
-        d_all(slot).wait_send()
+    d_all().wait_send()
+    t_all().wait_send()
+    for slot in turned:
+        turn_copy(slot, order[slot]).wait_send()
     for slot in range(1, passed + 1):
         y_copy(slot, order[slot]).wait_send()
     for wave in range(len(waves)):
@@ -504,7 +529,8 @@
             pltpu.VMEM((chans, width), BF16),
             *(pltpu.VMEM(t.shape, t.dtype) for t in held),
             pltpu.VMEM((inner_n, outer_n, 2 * per, tok), BF16),
-            pltpu.VMEM((inner_n // 2, outer_n, 2 * per, tok), BF16),
+            pltpu.VMEM((inner_n - 3, outer_n, 2 * per, tok), BF16),
+            pltpu.VMEM((2, outer_n, 2 * per, tok), BF16),
             pltpu.VMEM((outer_n, inner_n, 2 * per, tok), BF16),
             pltpu.VMEM((slabs * 2 * per, tok), F32),
             pltpu.VMEM((outer_n, per * inner_n, tok), BF16),
@@ -520,11 +546,12 @@
             pltpu.VMEM((chan_n, parts, width, each * slabs), BF16),
             pltpu.VMEM((width, piece), F32),
             dma((12,)),
-            pltpu.SemaphoreType.REGULAR,
             dma((inner_n,)),
             dma((inner_n,)),
-            dma((inner_n // 4,)),
-            dma((inner_n // 4,)),
+            dma((inner_n // 2 - 1,)),
+            dma((inner_n // 2 - 1,)),
+            dma((1,)),
+            dma((1,)),
             dma((inner_n,)),
             dma((inner_n,)),
             dma((inner_n,)),

time: 71.5 us -> 71.2 us (level)
  no operation moved by 1% of the time
where the time goes in v5:
time: 71.2 us; the launch traced here: 71 us
  Pallas kernels  69.3 us (97%)
  local copies, waits for them, and re-layouts  1.67 us (2%)
    pallas_call x1, Pallas kernels, local(): pl.pallas_call(functools.partial(kernel, sizes), out_shape=jax.ShapeDtype...  69.3 us
    unnamed x1, local copies, waits for them, and re-layouts  1.67 us

profile of v5, /device:TPU:1, one launch (start us, length us, event | category | flops | bytes accessed | tf_op | source)
XLA Modules:
  0.0 71.0 jit_solution(6316954054233121517)
XLA Ops:
  0.0 69.3 %shard_map.118 = bf16[256,512]{1,0:T(8,128)(2,1)} custom-call(bf16[128,1024]{1,0:T(8,128)(2,1)} %q_hbm.1, bf16[128,1024]{1,0:T(8,128)(2,1)} %k_hbm.1, bf16[128,1024]{1,0:T(8,128)(2,1)} %v_hbm.1, bf16[128,1024]{1,0:T(8,128)(2,1)} %taps_hbm.1, f32[1,1024]{1,0:T(1,128)} %bitcast.1, bf16[1024,512]{1,0:T(8,128)(2,1)} %w_hbm.1, ...), custom_call_target="tpu_custom_call" | custom-call | tf_op jit(solution)/shard_map/pallas_call | solution.py:519
  69.3 1.7 %copy.14 = bf16[256,512]{1,0:T(8,128)(2,1)} copy(bf16[256,512]{1,0:T(8,128)(2,1)} %shard_map.118) | data formatting | bytes 524288

commit v6 on v5

--- a/solution.py
+++ b/solution.py
@@ -78,11 +78,11 @@
     sizes,
     q_hbm, k_hbm, v_hbm, taps_hbm, skip_hbm, w_hbm,
     section_hbm, twist_hbm, forth_hbm, inverse_hbm, back_hbm, pick_hbm,
-    out_ref,
+    out_hbm,
     k_buf, v_buf, taps_buf, skip_ref, w_buf, section_ref, twist_ref, forth_ref, inverse_ref, back_ref, pick_ref,
     send1, recv1, middle, recv2, signals, send2, recv3, conv_rows, q_recv, gains, folded, gate_q,
-    gx, gated, w_rows, weights, total,
-    load_sem, y_send, y_recv, z_send, z_recv, t_send, t_recv, d_send, d_recv, q_send, q_recv_sem, b_send, b_recv, x_send, x_recv,
+    gx, gated, w_rows, weights, total, out_buf,
+    load_sem, out_sem, y_send, y_recv, z_send, z_recv, t_send, t_recv, d_send, d_recv, q_send, q_recv_sem, b_send, b_recv, x_send, x_recv,
     g_send, g_recv, w_send, w_recv, f_send, f_recv,
 ):
     outer_n, inner_n, chan_n, tok, per, parts = sizes
@@ -434,6 +434,10 @@
         gated[h, 0, :, i] = gx[h, c]
         for way in range(2):
             g_copy(way, h, 1, OWN).start()
+
+    def out_copy(low, step):
+        span = pl.ds(low, step)
+        return pltpu.make_async_copy(out_buf.at[:, span], out_hbm.at[:, span], out_sem.at[low // step])
 
     events = []
     for h in range(parts):
@@ -459,15 +463,20 @@
             if h == 0:
                 for d in range(1, chan_n):
                     f_copy(d, 1 - core).wait_recv()
-            part = None
-            for group in range(chan_n):
-                left, right = weights[group, h], gated[h, group].reshape(each * slabs, near * tok)
-                term = dot(left, right)
-                part = term if part is None else part + term
-            if h < parts - 1:
-                total[...] = part if h == 0 else total[...] + part
-            else:
-                out_ref[...] = (total[...] + part).T.astype(BF16)
+            width = total.shape[0]
+            step = width if h < parts - 1 else width // 2
+            for low in range(0, width, step):
+                span = pl.ds(low, step)
+                part = None
+                for group in range(chan_n):
+                    left, right = weights[group, h, span], gated[h, group].reshape(each * slabs, near * tok)
+                    term = dot(left, right)
+                    part = term if part is None else part + term
+                if h < parts - 1:
+                    total[...] = part if h == 0 else total[...] + part
+                else:
+                    out_buf[:, span] = (total[span, :] + part).T.astype(BF16)
+                    out_copy(low, step).start()
 
     d_all().wait_send()
     t_all().wait_send()
@@ -497,6 +506,8 @@
             g_copy(way, h, 1, OWN).wait_send()
             for r in range(1, reach(way, h) + 1):
                 g_copy(way, h, r, REST if r == 1 else WHOLE).wait_send()
+    for half in range(2):
+        out_copy(half * (total.shape[0] // 2), total.shape[0] // 2).wait()
 
 
 def local(q_stream, k_stream, v_stream, filter_taps, skip_gain, out_weight):
@@ -520,7 +531,7 @@
         functools.partial(kernel, sizes),
         out_shape=jax.ShapeDtypeStruct((piece, width), BF16),
         in_specs=[hbm] * 12,
-        out_specs=pl.BlockSpec(memory_space=pltpu.VMEM),
+        out_specs=hbm,
         scratch_shapes=[
             pltpu.VMEM((tok, chans), BF16),
             pltpu.VMEM((tok, chans), BF16),
@@ -545,7 +556,9 @@
             pltpu.VMEM((width // lanes, chans, lanes), F32),
             pltpu.VMEM((chan_n, parts, width, each * slabs), BF16),
             pltpu.VMEM((width, piece), F32),
+            pltpu.VMEM((piece, width), BF16),
             dma((12,)),
+            dma((2,)),
             dma((inner_n,)),
             dma((inner_n,)),
             dma((inner_n // 2 - 1,)),

time: 71.2 us -> 70.9 us (level)
  no operation moved by 1% of the time
where the time goes in v6:
time: 70.9 us; the launch traced here: 70.7 us
  Pallas kernels  69 us (97%)
  local copies, waits for them, and re-layouts  1.67 us (2%)
    pallas_call x1, Pallas kernels, local(): pl.pallas_call(functools.partial(kernel, sizes), out_shape=jax.ShapeDtype...  69 us
    unnamed x1, local copies, waits for them, and re-layouts  1.67 us

profile of v6, /device:TPU:1, one launch (start us, length us, event | category | flops | bytes accessed | tf_op | source)
XLA Modules:
  0.0 70.7 jit_solution(11506618182596780104)
XLA Ops:
  0.0 69.0 %shard_map.118 = bf16[256,512]{1,0:T(8,128)(2,1)} custom-call(bf16[128,1024]{1,0:T(8,128)(2,1)} %q_hbm.1, bf16[128,1024]{1,0:T(8,128)(2,1)} %k_hbm.1, bf16[128,1024]{1,0:T(8,128)(2,1)} %v_hbm.1, bf16[128,1024]{1,0:T(8,128)(2,1)} %taps_hbm.1, f32[1,1024]{1,0:T(1,128)} %bitcast.1, bf16[1024,512]{1,0:T(8,128)(2,1)} %w_hbm.1, ...), custom_call_target="tpu_custom_call" | custom-call | tf_op jit(solution)/shard_map/pallas_call | solution.py:530
  69.0 1.7 %copy.14 = bf16[256,512]{1,0:T(8,128)(2,1)} copy(bf16[256,512]{1,0:T(8,128)(2,1)} %shard_map.118) | data formatting | bytes 524288
